TPU v7x, 32 devices: a whole 2x2x4 slice. The times are simulated.
32 devices in a mesh: slab: 2 (over y), gx: 4 (over z), gy: 4 (over x, core).
Axes of the slice: x: 2, y: 2, z: 4, core: 2. Of those that a mesh axis runs over, the one named last changes fastest.
Arguments:
- unary_levels: int32 [8, 128, 128, 128], P(None, ('slab', 'gx'), 'gy'), parts along dimension 1, may hold values from -128 to 127
- affinity_levels: int32 [3, 128, 128, 128], P(None, ('slab', 'gx'), 'gy'), parts along dimension 1, may hold values from 0 to 255
Outputs:
- labeling: float32 [8, 128, 128, 128], P(None, ('slab', 'gx'), 'gy'), parts along dimension 1
There are 2 independent parts, one for each index of `slab`. A program takes and returns all parts, laid end to end along the dimension named above; each array names one. Nothing has to cross between parts.
All inputs are finite; a program needn't handle non-finite values.
Results may differ from a plain program's by a relative error of at most 0.00002.
Values sent between devices are 32-bit elements; how exact they have to be, the bound alone decides.
No kernel may reach another device: no remote copies, remote signals or barrier semaphores. Data moves between devices by JAX's collectives and lax.ppermute only.
A program may use at most 64 MiB of HBM per device.

v0:
```python
import jax
import jax.numpy as jnp
from jax import lax
from jax.sharding import PartitionSpec as P

ITERS = 3


network = [
    (0, 1),
    (2, 3),
    (4, 5),
    (6, 7),
    (0, 2),
    (1, 3),
    (4, 6),
    (5, 7),
    (1, 2),
    (5, 6),
    (0, 4),
    (1, 5),
    (2, 6),
    (3, 7),
    (2, 4),
    (3, 5),
    (1, 2),
    (3, 4),
    (5, 6),
]


def from_behind(value, axis, steps):
    count = lax.axis_size(axis)
    initial, last = (max(0, -steps), min(count, count - steps))
    return lax.ppermute(value, axis, [(source, source + steps) for source in range(initial, last)])


def simplex(values):
    entries = [values[k] for k in range(values.shape[0])]
    for first, second in network:
        larger = jnp.maximum(entries[first], entries[second])
        smaller = jnp.minimum(entries[first], entries[second])
        entries[first] = larger
        entries[second] = smaller
    running = entries[0]
    threshold = running - 1.0
    for k in range(1, len(entries)):
        running = running + entries[k]
        threshold = jnp.maximum(threshold, (running - 1.0) / float(k + 1))
    return jnp.maximum(values - threshold, 0.0)


def body(unary_levels, affinity_levels):
    step_size = 0.28
    label_costs = unary_levels.astype(jnp.float32) / 64.0
    bounds = 0.5 * (0.05 + 0.95 * affinity_levels.astype(jnp.float32) / 255.0)
    count_x = label_costs.shape[1]
    count_y = label_costs.shape[2]
    last_x = lax.axis_index("gx") == lax.axis_size("gx") - 1
    last_y = lax.axis_index("gy") == lax.axis_size("gy") - 1
    rows_x = lax.broadcasted_iota(jnp.int32, (1, count_x, 1, 1), 1)
    rows_y = lax.broadcasted_iota(jnp.int32, (1, 1, count_y, 1), 2)
    keep_rows = jnp.logical_or(rows_x < count_x - 1, jnp.logical_not(last_x))
    keep_cols = jnp.logical_or(rows_y < count_y - 1, jnp.logical_not(last_y))
    primal = simplex(-label_costs)
    lifted = primal
    dual_x = jnp.zeros_like(primal)
    dual_y = jnp.zeros_like(primal)
    dual_z = jnp.zeros_like(primal)
    for sweep in range(ITERS):
        border_x = from_behind(lifted[:, :1], "gx", -1)
        border_y = from_behind(lifted[:, :, :1], "gy", -1)
        ahead_x = jnp.concatenate([lifted[:, 1:], border_x], axis=1)
        ahead_y = jnp.concatenate([lifted[:, :, 1:], border_y], axis=2)
        diff_x = jnp.where(keep_rows, ahead_x - lifted, 0.0)
        diff_y = jnp.where(keep_cols, ahead_y - lifted, 0.0)
        diff_z = jnp.concatenate(
            [lifted[..., 1:] - lifted[..., :-1], jnp.zeros_like(lifted[..., :1])], axis=3
        )
        dual_x = jnp.clip(dual_x + step_size * diff_x, -bounds[0], bounds[0])
        dual_y = jnp.clip(dual_y + step_size * diff_y, -bounds[1], bounds[1])
        dual_z = jnp.clip(dual_z + step_size * diff_z, -bounds[2], bounds[2])
        prior_x = from_behind(dual_x[:, -1:], "gx", 1)
        prior_y = from_behind(dual_y[:, :, -1:], "gy", 1)
        behind_x = jnp.concatenate([prior_x, dual_x[:, :-1]], axis=1)
        behind_y = jnp.concatenate([prior_y, dual_y[:, :, :-1]], axis=2)
        behind_z = jnp.concatenate([jnp.zeros_like(dual_z[..., :1]), dual_z[..., :-1]], axis=3)
        adjoint = behind_x - dual_x + (behind_y - dual_y) + (behind_z - dual_z)
        updated = simplex(primal - step_size * (adjoint + label_costs))
        lifted = 2.0 * updated - primal
        primal = updated
    return primal


def solution(mesh):
    placed = (P(None, ("slab", "gx"), "gy", None), P(None, ("slab", "gx"), "gy", None))
    return jax.shard_map(
        body,
        mesh=mesh,
        in_specs=placed,
        out_specs=P(None, ("slab", "gx"), "gy", None),
        check_vma=False,
    )
```

profile of v0, /device:TPU:9, one launch (start us, length us, event | category | flops | bytes accessed | tf_op | source)
XLA Modules:
  0.0 80.6 jit_solution(8221334729223796332)
XLA Ops:
  0.0 1.8 %fusion.43 = f32[8,16,32,128]{3,2,1,0:T(8,128)S(1)} fusion(s32[8,16,32,128]{3,2,1,0:T(8,128)} %param.2), kind=kLoop, calls=%fused_computation.68 | loop fusion | flops 1572864 | bytes 4194304 | tf_op jit(solution)/shard_map/neg | solution.py:65
  1.9 0.6 maximum_bitcast_fusion.3
  2.4 1.0 %copy-done = s32[8,16,32,128]{3,2,1,0:T(8,128)S(1)} copy-done((s32[8,16,32,128]{3,2,1,0:T(8,128)S(1)}, s32[8,16,32,128]{3,2,1,0:T(8,128)}, u32[]{:S(2)}) %copy-start) | copy-done | bytes 2097176
  3.4 0.3 subtract_maximum_fusion.3
  3.8 0.7 slice.297
  4.5 1.9 %collective-permute-start = (f32[8,1,32,128]{3,2,1,0:T(8,128)}, f32[8,1,32,128]{3,2,1,0:T(8,128)S(1)}, u32[]{:S(2)}, u32[]{:S(2)}) collective-permute-start(f32[8,1,32,128]{3,2,1,0:T(8,128)} %slice.297), channel_id=1, source_target_pairs={{4,0},{8,4},{12,8},{5,1},{9,5},{13,9},{6,2},{10,6},{14,10},{7,3},{... | collective-permute-start | bytes 393224 | tf_op jit(solution)/shard_map/ppermute | solution.py:35
  6.4 0.7 slice.302
  7.1 2.6 %collective-permute-start.2 = (f32[8,16,1,128]{3,2,1,0:T(1,128)}, f32[8,16,1,128]{3,2,1,0:T(1,128)}, u32[]{:S(2)}, u32[]{:S(2)}) collective-permute-start(f32[8,16,1,128]{3,2,1,0:T(1,128)} %slice.302), channel_id=1, source_target_pairs={{1,0},{2,1},{3,2},{5,4},{6,5},{7,6},{9,8},{10,9},{11,10},{13,12},{... | collective-permute-start | bytes 196616 | tf_op jit(solution)/shard_map/ppermute | solution.py:35
  9.7 1.9 %slice_subtract_fusion.2 = f32[8,16,32,127]{3,2,1,0:T(8,128)} fusion(f32[8,16,32,128]{3,2,1,0:T(8,128)S(1)} %subtract_maximum_fusion.3), kind=kLoop, calls=%fused_computation.2 | loop fusion | flops 520192 | bytes 6242304 | tf_op jit(solution)/shard_map/sub | solution.py:78
  11.8 1.0 %slice_bitcast_fusion = (f32[16,32,128]{2,1,0:T(8,128)S(1)}, f32[16,32,128]{2,1,0:T(8,128)S(1)}, f32[16,32,128]{2,1,0:T(8,128)S(1)}, f32[16,32,128]{2,1,0:T(8,12...) fusion(f32[3,16,32,128]{3,2,1,0:T(8,128)S(1)} %add_multiply_fusion), kind=kLoop, calls=%fused_computation.77 | loop fusion | flops 196608 | bytes 2359296 | tf_op jit(solution)/shard_map/jit(clip)/min | solution.py:82
  12.8 3.4 %slice.301 = f32[8,16,31,128]{3,2,1,0:T(8,128)} slice(f32[8,16,32,128]{3,2,1,0:T(8,128)} %copy-done.1), slice={[0:8], [0:16], [1:32], [0:128]} | slice | bytes 4063232 | tf_op jit(solution)/shard_map/slice | solution.py:74
  16.2 1.5 %slice.296 = f32[8,15,32,128]{3,2,1,0:T(8,128)} slice(f32[8,16,32,128]{3,2,1,0:T(8,128)S(1)} %copy-done.2), slice={[0:8], [1:16], [0:32], [0:128]} | slice | bytes 3932160 | tf_op jit(solution)/shard_map/slice | solution.py:73
  17.7 3.6 %fusion.12 = (f32[8,16,32,128]{3,2,1,0:T(8,128)S(1)}, f32[8,16,32,128]{3,2,1,0:T(8,128)S(1)}) fusion(f32[8,16,1,128]{3,2,1,0:T(1,128)} %collective-permute-done.2, f32[8,16,31,128]{3,2,1,0:T(8,128)} %slice.301, f32[16,32,128]{2,1,0:T(8,128)S(1)} %get-tuple-element.13, f32[16,32,128]{2,1,0:T(8,128)} %get-tuple-element.15, ...), kind=kLoop, calls=%fused_computation.18 | loop fusion | flops 8912896 | bytes 11796528 | tf_op jit(solution)/shard_map/jit(clip)/min | solution.py:81
  21.3 3.6 %collective-permute-start.1 = (f32[8,1,32,128]{3,2,1,0:T(8,128)S(1)}, f32[8,1,32,128]{3,2,1,0:T(8,128)S(1)}, u32[]{:S(2)}, u32[]{:S(2)}) collective-permute-start(f32[8,1,32,128]{3,2,1,0:T(8,128)S(1)} %slice.298), channel_id=1, source_target_pairs={{0,4},{4,8},{8,12},{1,5},{5,9},{9,13},{2,6},{6,10},{10,14},{3,7},{... | collective-permute-start | bytes 393224 | tf_op jit(solution)/shard_map/ppermute | solution.py:35
  25.1 3.3 %collective-permute-start.3 = (f32[8,16,1,128]{3,2,1,0:T(1,128)S(1)}, f32[8,16,1,128]{3,2,1,0:T(1,128)S(1)}, u32[]{:S(2)}, u32[]{:S(2)}) collective-permute-start(f32[8,16,1,128]{3,2,1,0:T(1,128)S(1)} %slice.303), channel_id=1, source_target_pairs={{0,1},{1,2},{2,3},{4,5},{5,6},{6,7},{8,9},{9,10},{10,11},{12,13},{... | collective-permute-start | bytes 196616 | tf_op jit(solution)/shard_map/ppermute | solution.py:35
  28.4 0.3 maximum_minimum_fusion.2
  28.9 0.7 collective-permute-done.3
  29.7 2.0 %fusion.8 = f32[8,16,32,128]{3,2,1,0:T(8,128)S(1)} fusion(f32[8,16,32,128]{3,2,1,0:T(8,128)S(1)} %get-tuple-element.6, f32[8,15,32,128]{3,2,1,0:T(8,128)S(1)} %slice.299, f32[8,1,32,128]{3,2,1,0:T(8,128)S(1)} %collective-permute-done.1, f32[8,16,32,128]{3,2,1,0:T(8,128)S(1)} %get-tuple-element.5, f32[8,16,31,128]{3,2,1,0:T(8,128)S(1)} %bitcast.27, ...), kind=kLoop, calls=%fused_computation.13 | loop fusion | flops 9437184 | bytes 17530880 | tf_op jit(solution)/shard_map/sub | solution.py:89
  31.7 0.6 maximum_bitcast_fusion.2
  32.3 0.6 multiply_subtract_fusion.1
  33.0 2.1 %collective-permute-start.4 = (f32[8,1,32,128]{3,2,1,0:T(8,128)S(1)}, f32[8,1,32,128]{3,2,1,0:T(8,128)S(1)}, u32[]{:S(2)}, u32[]{:S(2)}) collective-permute-start(f32[8,1,32,128]{3,2,1,0:T(8,128)S(1)} %slice.318), channel_id=1, source_target_pairs={{4,0},{8,4},{12,8},{5,1},{9,5},{13,9},{6,2},{10,6},{14,10},{7,3},{... | collective-permute-start | bytes 393224 | tf_op jit(solution)/shard_map/ppermute | solution.py:35
  35.1 1.9 %collective-permute-start.6 = (f32[8,16,1,128]{3,2,1,0:T(1,128)S(1)}, f32[8,16,1,128]{3,2,1,0:T(1,128)S(1)}, u32[]{:S(2)}, u32[]{:S(2)}) collective-permute-start(f32[8,16,1,128]{3,2,1,0:T(1,128)S(1)} %slice.322), channel_id=1, source_target_pairs={{1,0},{2,1},{3,2},{5,4},{6,5},{7,6},{9,8},{10,9},{11,10},{13,12},{... | collective-permute-start | bytes 196616 | tf_op jit(solution)/shard_map/ppermute | solution.py:35
  37.0 0.6 slice_subtract_fusion.1
  37.7 0.4 slice.321
  38.0 1.5 %slice.317 = f32[8,15,32,128]{3,2,1,0:T(8,128)} slice(f32[8,16,32,128]{3,2,1,0:T(8,128)S(1)} %multiply_subtract_fusion.1), slice={[0:8], [1:16], [0:32], [0:128]} | slice | bytes 3932160 | tf_op jit(solution)/shard_map/slice | solution.py:73
  39.5 2.1 %collective-permute-done.6 = f32[8,16,1,128]{3,2,1,0:T(1,128)S(1)} collective-permute-done((f32[8,16,1,128]{3,2,1,0:T(1,128)S(1)}, f32[8,16,1,128]{3,2,1,0:T(1,128)S(1)}, u32[]{:S(2)}, u32[]{:S(2)}) %collective-permute-start.6) | collective-permute-done | bytes 65568 | tf_op jit(solution)/shard_map/ppermute | solution.py:35
  41.6 3.1 %fusion.27 = (f32[8,16,32,128]{3,2,1,0:T(8,128)S(1)}, f32[8,16,32,128]{3,2,1,0:T(8,128)S(1)}) fusion(f32[8,16,32,128]{3,2,1,0:T(8,128)S(1)} %get-tuple-element.5, f32[8,16,32,128]{3,2,1,0:T(8,128)S(1)} %multiply_subtract_fusion.1, f32[8,16,1,128]{3,2,1,0:T(1,128)S(1)} %collective-permute-done.6, f32[8,16,31,128]{3,2,1,0:T(8,128)S(1)} %slice.321, ...), kind=kLoop, calls=%fused_computation.37 | loop fusion | flops 7340032 | bytes 15728688 | tf_op jit(solution)/shard_map/jit(clip)/min | solution.py:81
  44.7 3.2 %collective-permute-start.5 = (f32[8,1,32,128]{3,2,1,0:T(8,128)S(1)}, f32[8,1,32,128]{3,2,1,0:T(8,128)S(1)}, u32[]{:S(2)}, u32[]{:S(2)}) collective-permute-start(f32[8,1,32,128]{3,2,1,0:T(8,128)S(1)} %slice.319), channel_id=1, source_target_pairs={{0,4},{4,8},{8,12},{1,5},{5,9},{9,13},{2,6},{6,10},{10,14},{3,7},{... | collective-permute-start | bytes 393224 | tf_op jit(solution)/shard_map/ppermute | solution.py:35
  48.0 3.0 %collective-permute-start.7 = (f32[8,16,1,128]{3,2,1,0:T(1,128)S(1)}, f32[8,16,1,128]{3,2,1,0:T(1,128)S(1)}, u32[]{:S(2)}, u32[]{:S(2)}) collective-permute-start(f32[8,16,1,128]{3,2,1,0:T(1,128)S(1)} %slice.323), channel_id=1, source_target_pairs={{0,1},{1,2},{2,3},{4,5},{5,6},{6,7},{8,9},{9,10},{10,11},{12,13},{... | collective-permute-start | bytes 196616 | tf_op jit(solution)/shard_map/ppermute | solution.py:35
  51.0 0.6 maximum_minimum_fusion.1
  52.2 3.1 %fusion.22 = f32[8,16,32,128]{3,2,1,0:T(8,128)S(1)} fusion(f32[8,16,32,128]{3,2,1,0:T(8,128)S(1)} %get-tuple-element.10, f32[8,15,32,128]{3,2,1,0:T(8,128)S(1)} %slice.320, f32[8,1,32,128]{3,2,1,0:T(8,128)S(1)} %collective-permute-done.5, f32[8,16,32,128]{3,2,1,0:T(8,128)S(1)} %get-tuple-element.9, f32[8,16,31,128]{3,2,1,0:T(8,128)S(1)} %bitcast.26, ...), kind=kLoop, calls=%fused_computation.31 | loop fusion | flops 7340032 | bytes 19120128 | tf_op jit(solution)/shard_map/sub | solution.py:89
  55.3 0.6 maximum_bitcast_fusion.1
  55.9 0.4 copy-done.8
  56.2 0.6 multiply_subtract_fusion
  57.0 2.1 %collective-permute-start.8 = (f32[8,1,32,128]{3,2,1,0:T(8,128)S(1)}, f32[8,1,32,128]{3,2,1,0:T(8,128)S(1)}, u32[]{:S(2)}, u32[]{:S(2)}) collective-permute-start(f32[8,1,32,128]{3,2,1,0:T(8,128)S(1)} %slice.337), channel_id=1, source_target_pairs={{4,0},{8,4},{12,8},{5,1},{9,5},{13,9},{6,2},{10,6},{14,10},{7,3},{... | collective-permute-start | bytes 393224 | tf_op jit(solution)/shard_map/ppermute | solution.py:35
  59.1 1.9 %collective-permute-start.10 = (f32[8,16,1,128]{3,2,1,0:T(1,128)S(1)}, f32[8,16,1,128]{3,2,1,0:T(1,128)S(1)}, u32[]{:S(2)}, u32[]{:S(2)}) collective-permute-start(f32[8,16,1,128]{3,2,1,0:T(1,128)S(1)} %slice.341), channel_id=1, source_target_pairs={{1,0},{2,1},{3,2},{5,4},{6,5},{7,6},{9,8},{10,9},{11,10},{13,12},{... | collective-permute-start | bytes 196616 | tf_op jit(solution)/shard_map/ppermute | solution.py:35
  61.1 0.6 slice_subtract_fusion
  61.7 0.4 slice.340
  62.0 1.5 %slice.336 = f32[8,15,32,128]{3,2,1,0:T(8,128)} slice(f32[8,16,32,128]{3,2,1,0:T(8,128)S(1)} %multiply_subtract_fusion), slice={[0:8], [1:16], [0:32], [0:128]} | slice | bytes 3932160 | tf_op jit(solution)/shard_map/slice | solution.py:73
  63.5 2.1 %collective-permute-done.10 = f32[8,16,1,128]{3,2,1,0:T(1,128)S(1)} collective-permute-done((f32[8,16,1,128]{3,2,1,0:T(1,128)S(1)}, f32[8,16,1,128]{3,2,1,0:T(1,128)S(1)}, u32[]{:S(2)}, u32[]{:S(2)}) %collective-permute-start.10) | collective-permute-done | bytes 65568 | tf_op jit(solution)/shard_map/ppermute | solution.py:35
  65.6 3.1 %fusion.42 = (f32[8,16,32,128]{3,2,1,0:T(8,128)S(1)}, f32[8,16,32,128]{3,2,1,0:T(8,128)S(1)}) fusion(f32[8,16,32,128]{3,2,1,0:T(8,128)S(1)} %get-tuple-element.9, f32[8,16,32,128]{3,2,1,0:T(8,128)S(1)} %multiply_subtract_fusion, f32[8,16,1,128]{3,2,1,0:T(1,128)S(1)} %collective-permute-done.10, f32[8,16,31,128]{3,2,1,0:T(8,128)S(1)} %slice.340, ...), kind=kLoop, calls=%fused_computation.56 | loop fusion | flops 7340032 | bytes 15728688 | tf_op jit(solution)/shard_map/jit(clip)/min | solution.py:81
  68.7 3.2 %collective-permute-start.9 = (f32[8,1,32,128]{3,2,1,0:T(8,128)S(1)}, f32[8,1,32,128]{3,2,1,0:T(8,128)S(1)}, u32[]{:S(2)}, u32[]{:S(2)}) collective-permute-start(f32[8,1,32,128]{3,2,1,0:T(8,128)S(1)} %slice.338), channel_id=1, source_target_pairs={{0,4},{4,8},{8,12},{1,5},{5,9},{9,13},{2,6},{6,10},{10,14},{3,7},{... | collective-permute-start | bytes 393224 | tf_op jit(solution)/shard_map/ppermute | solution.py:35
  72.0 2.8 %collective-permute-start.11 = (f32[8,16,1,128]{3,2,1,0:T(1,128)S(1)}, f32[8,16,1,128]{3,2,1,0:T(1,128)S(1)}, u32[]{:S(2)}, u32[]{:S(2)}) collective-permute-start(f32[8,16,1,128]{3,2,1,0:T(1,128)S(1)} %slice.342), channel_id=1, source_target_pairs={{0,1},{1,2},{2,3},{4,5},{5,6},{6,7},{8,9},{9,10},{10,11},{12,13},{... | collective-permute-start | bytes 196616 | tf_op jit(solution)/shard_map/ppermute | solution.py:35
  74.8 0.6 maximum_minimum_fusion
  75.6 0.5 collective-permute-done.11
  76.3 2.1 %fusion.37 = f32[8,16,32,128]{3,2,1,0:T(8,128)S(1)} fusion(f32[8,16,32,128]{3,2,1,0:T(8,128)S(1)} %get-tuple-element.8, f32[8,15,32,128]{3,2,1,0:T(8,128)S(1)} %slice.339, f32[8,1,32,128]{3,2,1,0:T(8,128)S(1)} %collective-permute-done.9, f32[8,16,32,128]{3,2,1,0:T(8,128)S(1)} %get-tuple-element.7, f32[8,16,31,128]{3,2,1,0:T(8,128)S(1)} %bitcast.29, ...), kind=kLoop, calls=%fused_computation.50 | loop fusion | flops 7340032 | bytes 19120128 | tf_op jit(solution)/shard_map/sub | solution.py:89
  78.5 0.6 maximum_bitcast_fusion
  79.0 1.6 %subtract_maximum_fusion = f32[8,16,32,128]{3,2,1,0:T(8,128)} fusion(f32[8,16,32,128]{3,2,1,0:T(8,128)S(1)} %fusion.37, f32[16,32,128]{2,1,0:T(8,128)S(1)} %maximum_bitcast_fusion), kind=kLoop, calls=%fused_computation.58 | loop fusion | flops 1048576 | bytes 4456448 | tf_op jit(solution)/shard_map/max | solution.py:50
  (46 shorter events, 1.9 us)
Async XLA Ops:
  1.8 1.6 %copy-start = (s32[8,16,32,128]{3,2,1,0:T(8,128)S(1)}, s32[8,16,32,128]{3,2,1,0:T(8,128)}, u32[]{:S(2)}) copy-start(s32[8,16,32,128]{3,2,1,0:T(8,128)} %param.2) | copy-start | bytes 6291460
  3.8 7.9 %copy-start.1 = (f32[8,16,32,128]{3,2,1,0:T(8,128)}, f32[8,16,32,128]{3,2,1,0:T(8,128)S(1)}, u32[]{:S(2)}) copy-start(f32[8,16,32,128]{3,2,1,0:T(8,128)S(1)} %subtract_maximum_fusion.3) | copy-start | bytes 6291460
  4.5 13.2 %collective-permute-start = (f32[8,1,32,128]{3,2,1,0:T(8,128)}, f32[8,1,32,128]{3,2,1,0:T(8,128)S(1)}, u32[]{:S(2)}, u32[]{:S(2)}) collective-permute-start(f32[8,1,32,128]{3,2,1,0:T(8,128)} %slice.297), channel_id=1, source_target_pairs={{4,0},{8,4},{12,8},{5,1},{9,5},{13,9},{6,2},{10,6},{14,10},{7,3},{... | collective-permute-start | bytes 393224 | tf_op jit(solution)/shard_map/ppermute | solution.py:35
  7.1 10.6 %collective-permute-start.2 = (f32[8,16,1,128]{3,2,1,0:T(1,128)}, f32[8,16,1,128]{3,2,1,0:T(1,128)}, u32[]{:S(2)}, u32[]{:S(2)}) collective-permute-start(f32[8,16,1,128]{3,2,1,0:T(1,128)} %slice.302), channel_id=1, source_target_pairs={{1,0},{2,1},{3,2},{5,4},{6,5},{7,6},{9,8},{10,9},{11,10},{13,12},{... | collective-permute-start | bytes 196616 | tf_op jit(solution)/shard_map/ppermute | solution.py:35
  9.7 2.0 %copy-start.11 = (s32[3,16,32,128]{3,2,1,0:T(8,128)S(1)}, s32[3,16,32,128]{3,2,1,0:T(8,128)}, u32[]{:S(2)}) copy-start(s32[3,16,32,128]{3,2,1,0:T(8,128)} %param.3) | copy-start | bytes 2359300
  12.8 3.4 %copy-start.2 = (f32[8,16,32,128]{3,2,1,0:T(8,128)S(1)}, f32[8,16,32,128]{3,2,1,0:T(8,128)}, u32[]{:S(2)}) copy-start(f32[8,16,32,128]{3,2,1,0:T(8,128)} %copy-done.1) | copy-start | bytes 6291460
  17.7 10.6 %copy-start.3 = (f32[8,16,32,127]{3,2,1,0:T(8,128)S(1)}, f32[8,16,32,127]{3,2,1,0:T(8,128)}, u32[]{:S(2)}) copy-start(f32[8,16,32,127]{3,2,1,0:T(8,128)} %slice_subtract_fusion.2) | copy-start | bytes 6242308
  21.3 8.3 %collective-permute-start.1 = (f32[8,1,32,128]{3,2,1,0:T(8,128)S(1)}, f32[8,1,32,128]{3,2,1,0:T(8,128)S(1)}, u32[]{:S(2)}, u32[]{:S(2)}) collective-permute-start(f32[8,1,32,128]{3,2,1,0:T(8,128)S(1)} %slice.298), channel_id=1, source_target_pairs={{0,4},{4,8},{8,12},{1,5},{5,9},{9,13},{2,6},{6,10},{10,14},{3,7},{... | collective-permute-start | bytes 393224 | tf_op jit(solution)/shard_map/ppermute | solution.py:35
  25.1 4.6 %collective-permute-start.3 = (f32[8,16,1,128]{3,2,1,0:T(1,128)S(1)}, f32[8,16,1,128]{3,2,1,0:T(1,128)S(1)}, u32[]{:S(2)}, u32[]{:S(2)}) collective-permute-start(f32[8,16,1,128]{3,2,1,0:T(1,128)S(1)} %slice.303), channel_id=1, source_target_pairs={{0,1},{1,2},{2,3},{4,5},{5,6},{6,7},{8,9},{9,10},{10,11},{12,13},{... | collective-permute-start | bytes 196616 | tf_op jit(solution)/shard_map/ppermute | solution.py:35
  32.2 0.7 copy-start.7
  33.0 8.6 %collective-permute-start.4 = (f32[8,1,32,128]{3,2,1,0:T(8,128)S(1)}, f32[8,1,32,128]{3,2,1,0:T(8,128)S(1)}, u32[]{:S(2)}, u32[]{:S(2)}) collective-permute-start(f32[8,1,32,128]{3,2,1,0:T(8,128)S(1)} %slice.318), channel_id=1, source_target_pairs={{4,0},{8,4},{12,8},{5,1},{9,5},{13,9},{6,2},{10,6},{14,10},{7,3},{... | collective-permute-start | bytes 393224 | tf_op jit(solution)/shard_map/ppermute | solution.py:35
  35.1 6.5 %collective-permute-start.6 = (f32[8,16,1,128]{3,2,1,0:T(1,128)S(1)}, f32[8,16,1,128]{3,2,1,0:T(1,128)S(1)}, u32[]{:S(2)}, u32[]{:S(2)}) collective-permute-start(f32[8,16,1,128]{3,2,1,0:T(1,128)S(1)} %slice.322), channel_id=1, source_target_pairs={{1,0},{2,1},{3,2},{5,4},{6,5},{7,6},{9,8},{10,9},{11,10},{13,12},{... | collective-permute-start | bytes 196616 | tf_op jit(solution)/shard_map/ppermute | solution.py:35
  38.0 3.6 %copy-start.4 = (f32[16,32,128]{2,1,0:T(8,128)S(1)}, f32[16,32,128]{2,1,0:T(8,128)}, u32[]{:S(2)}) copy-start(f32[16,32,128]{2,1,0:T(8,128)} %get-tuple-element.15) | copy-start | bytes 786436
  38.0 3.6 %copy-start.5 = (f32[16,32,128]{2,1,0:T(8,128)S(1)}, f32[16,32,128]{2,1,0:T(8,128)}, u32[]{:S(2)}) copy-start(f32[16,32,128]{2,1,0:T(8,128)} %get-tuple-element.16) | copy-start | bytes 786436
  44.7 7.4 %collective-permute-start.5 = (f32[8,1,32,128]{3,2,1,0:T(8,128)S(1)}, f32[8,1,32,128]{3,2,1,0:T(8,128)S(1)}, u32[]{:S(2)}, u32[]{:S(2)}) collective-permute-start(f32[8,1,32,128]{3,2,1,0:T(8,128)S(1)} %slice.319), channel_id=1, source_target_pairs={{0,4},{4,8},{8,12},{1,5},{5,9},{9,13},{2,6},{6,10},{10,14},{3,7},{... | collective-permute-start | bytes 393224 | tf_op jit(solution)/shard_map/ppermute | solution.py:35
  48.0 4.1 %collective-permute-start.7 = (f32[8,16,1,128]{3,2,1,0:T(1,128)S(1)}, f32[8,16,1,128]{3,2,1,0:T(1,128)S(1)}, u32[]{:S(2)}, u32[]{:S(2)}) collective-permute-start(f32[8,16,1,128]{3,2,1,0:T(1,128)S(1)} %slice.323), channel_id=1, source_target_pairs={{0,1},{1,2},{2,3},{4,5},{5,6},{6,7},{8,9},{9,10},{10,11},{12,13},{... | collective-permute-start | bytes 196616 | tf_op jit(solution)/shard_map/ppermute | solution.py:35
  55.3 1.0 %copy-start.8 = (f32[16,32,128]{2,1,0:T(8,128)S(1)}, f32[16,32,128]{2,1,0:T(8,128)}, u32[]{:S(2)}) copy-start(f32[16,32,128]{2,1,0:T(8,128)} %copy-done.7) | copy-start | bytes 786436
  56.2 0.7 copy-start.9
  57.0 8.6 %collective-permute-start.8 = (f32[8,1,32,128]{3,2,1,0:T(8,128)S(1)}, f32[8,1,32,128]{3,2,1,0:T(8,128)S(1)}, u32[]{:S(2)}, u32[]{:S(2)}) collective-permute-start(f32[8,1,32,128]{3,2,1,0:T(8,128)S(1)} %slice.337), channel_id=1, source_target_pairs={{4,0},{8,4},{12,8},{5,1},{9,5},{13,9},{6,2},{10,6},{14,10},{7,3},{... | collective-permute-start | bytes 393224 | tf_op jit(solution)/shard_map/ppermute | solution.py:35
  59.1 6.5 %collective-permute-start.10 = (f32[8,16,1,128]{3,2,1,0:T(1,128)S(1)}, f32[8,16,1,128]{3,2,1,0:T(1,128)S(1)}, u32[]{:S(2)}, u32[]{:S(2)}) collective-permute-start(f32[8,16,1,128]{3,2,1,0:T(1,128)S(1)} %slice.341), channel_id=1, source_target_pairs={{1,0},{2,1},{3,2},{5,4},{6,5},{7,6},{9,8},{10,9},{11,10},{13,12},{... | collective-permute-start | bytes 196616 | tf_op jit(solution)/shard_map/ppermute | solution.py:35
  62.0 3.6 %copy-start.6 = (f32[16,32,128]{2,1,0:T(8,128)S(1)}, f32[16,32,128]{2,1,0:T(8,128)}, u32[]{:S(2)}) copy-start(f32[16,32,128]{2,1,0:T(8,128)} %get-tuple-element.16) | copy-start | bytes 786436
  68.7 7.4 %collective-permute-start.9 = (f32[8,1,32,128]{3,2,1,0:T(8,128)S(1)}, f32[8,1,32,128]{3,2,1,0:T(8,128)S(1)}, u32[]{:S(2)}, u32[]{:S(2)}) collective-permute-start(f32[8,1,32,128]{3,2,1,0:T(8,128)S(1)} %slice.338), channel_id=1, source_target_pairs={{0,4},{4,8},{8,12},{1,5},{5,9},{9,13},{2,6},{6,10},{10,14},{3,7},{... | collective-permute-start | bytes 393224 | tf_op jit(solution)/shard_map/ppermute | solution.py:35
  72.0 4.1 %collective-permute-start.11 = (f32[8,16,1,128]{3,2,1,0:T(1,128)S(1)}, f32[8,16,1,128]{3,2,1,0:T(1,128)S(1)}, u32[]{:S(2)}, u32[]{:S(2)}) collective-permute-start(f32[8,16,1,128]{3,2,1,0:T(1,128)S(1)} %slice.342), channel_id=1, source_target_pairs={{0,1},{1,2},{2,3},{4,5},{5,6},{6,7},{8,9},{9,10},{10,11},{12,13},{... | collective-permute-start | bytes 196616 | tf_op jit(solution)/shard_map/ppermute | solution.py:35
  75.4 1.0 %copy-start.10 = (f32[16,32,128]{2,1,0:T(8,128)S(1)}, f32[16,32,128]{2,1,0:T(8,128)}, u32[]{:S(2)}) copy-start(f32[16,32,128]{2,1,0:T(8,128)} %copy-done.9) | copy-start | bytes 786436
where the time goes:
time: 82.2 us; the launch traced here: 80.6 us
  starting transfers between devices  31.6 us (38%)
  other arithmetic  30.1 us (37%)
  local copies, waits for them, and re-layouts  12.8 us (16%)
  waiting for transfers between devices  5.7 us (7%)
    ppermute x12, starting transfers between devices, from_behind(): lax.ppermute(value, axis, [(source, source + steps) for source in range(i...  31.6 us
    min x3, other arithmetic, body(): dual_y = jnp.clip(dual_y + step_size * diff_y, -bounds[1], bounds[1])  9.75 us
    sub x3, other arithmetic, body(): updated = simplex(primal - step_size * (adjoint + label_costs))  7.22 us
    ppermute x12, waiting for transfers between devices, from_behind(): lax.ppermute(value, axis, [(source, source + steps) for source in range(i...  5.7 us
    slice x3, local copies, waits for them, and re-layouts, body(): ahead_x = jnp.concatenate([lifted[:, 1:], border_x], axis=1)  4.42 us
    slice x3, local copies, waits for them, and re-layouts, body(): ahead_y = jnp.concatenate([lifted[:, :, 1:], border_y], axis=2)  4.12 us
    sub x3, other arithmetic, body(): lifted[..., 1:] - lifted[..., :-1]  3.15 us
    min x4, other arithmetic, body(): dual_z = jnp.clip(dual_z + step_size * diff_z, -bounds[2], bounds[2])  2.59 us
  transfers between devices with their start and end apart: 12, of which 5 were waited for; matrix products, arithmetic and copies ran while one was open for 20% of the time, Pallas kernels for 0%

commit v1 on v0

v1 whole, which is shorter than its diff:
```python
import functools

import jax
import jax.numpy as jnp
from jax import lax
from jax.experimental import pallas as pl
from jax.experimental.pallas import tpu as pltpu
from jax.sharding import PartitionSpec as P

STEP = 0.28
LABELS = 8
COSTS = LABELS - 1
FIELDS = COSTS + 3
HALO = 3
ROWS = 8
LANES = 128
COST_SCALE = STEP / 64.0

NETWORK = [
    (0, 1), (2, 3), (4, 5), (6, 7),
    (0, 2), (1, 3), (4, 6), (5, 7),
    (1, 2), (5, 6),
    (0, 4), (1, 5), (2, 6), (3, 7),
    (2, 4), (3, 5),
    (1, 2), (3, 4), (5, 6),
]

VM = pl.BlockSpec(memory_space=pltpu.VMEM)
HB = pl.BlockSpec(memory_space=pltpu.HBM)


def params(mebibytes=8):
    return pltpu.CompilerParams(vmem_limit_bytes=mebibytes << 20)


def matching(count, first):
    pairs = []
    for low in range(first, count - 1, 2):
        pairs += [(low, low + 1), (low + 1, low)]
    return pairs


def swap(value, axis, first):
    return lax.ppermute(value, axis, matching(lax.axis_size(axis), first))


def simplex(values):
    s = list(values)
    for a, b in NETWORK:
        s[a], s[b] = jnp.maximum(s[a], s[b]), jnp.minimum(s[a], s[b])
    running = s[0] - 1.0
    threshold = running
    for k in range(1, len(s)):
        running = running + s[k]
        threshold = jnp.maximum(threshold, running * (1.0 / (k + 1)))
    return [jnp.maximum(v - threshold, 0.0) for v in values]


def bound_of(levels):
    return (0.5 / STEP) * (0.05 + 0.95 / 255.0 * levels.astype(jnp.float32))


def edge_kernel(nx, u_hbm, a_hbm, m0, m1, ubuf, abuf, sems):
    copies = []
    for side, start in enumerate((0, nx - HALO)):
        copies.append(pltpu.make_async_copy(u_hbm.at[:, pl.ds(start, HALO)], ubuf.at[side], sems.at[2 * side]))
        copies.append(pltpu.make_async_copy(a_hbm.at[:, pl.ds(start, HALO)], abuf.at[side], sems.at[2 * side + 1]))
    for c in copies:
        c.start()
    for c in copies:
        c.wait()
    odd = lax.rem(lax.axis_index("gx"), 2)
    last_y = lax.axis_index("gy") == lax.axis_size("gy") - 1
    plane = u_hbm.shape[2:]
    row = lax.broadcasted_iota(jnp.int32, plane, 0)
    lane = lax.broadcasted_iota(jnp.int32, plane, 1)
    keep_y = jnp.logical_or(row < plane[0] - 1, jnp.logical_not(last_y))
    keep_z = lane < LANES - 1
    for m, side in ((m0, 1 - odd), (m1, odd)):
        for d in range(HALO):
            last = ubuf[side, LABELS - 1, d]
            for k in range(COSTS):
                m[d * COSTS + k] = (ubuf[side, k, d] - last).astype(jnp.float32) * COST_SCALE
            m[HALO * COSTS + d] = bound_of(abuf[side, 0, d])
        for d in range(HALO - 1):
            for axis, keep in ((1, keep_y), (2, keep_z)):
                value = jnp.where(keep, bound_of(abuf[side, axis, d + side]), 0.0)
                m[HALO * (COSTS + 1) + 2 * d + axis - 1] = value


def main_kernel(nx, ny, u_hbm, a_hbm, after, costs, bounds, y0, y1, ubuf, abuf, sems):
    chunk = nx // 4
    copies = []
    for c in range(4):
        part = pl.ds(c * chunk, chunk)
        copies.append((
            pltpu.make_async_copy(u_hbm.at[:, part], ubuf.at[:, part], sems.at[2 * c]),
            pltpu.make_async_copy(a_hbm.at[:, part], abuf.at[:, part], sems.at[2 * c + 1]),
        ))
    for pair in copies:
        for c in pair:
            c.start()
    last_x = lax.axis_index("gx") == lax.axis_size("gx") - 1
    last_y = lax.axis_index("gy") == lax.axis_size("gy") - 1
    odd = lax.rem(lax.axis_index("gy"), 2)
    row = lax.broadcasted_iota(jnp.int32, (ny, LANES), 0)
    lane = lax.broadcasted_iota(jnp.int32, (ny, LANES), 1)
    keep_y = jnp.logical_or(row < ny - 1, jnp.logical_not(last_y))
    keep_z = lane < LANES - 1
    zero = jnp.zeros((ROWS, LANES), jnp.float32)

    def layer(x, _):
        last = ubuf[LABELS - 1, x]
        for k in range(COSTS):
            costs[x + HALO, k, 0:ny] = (ubuf[k, x] - last).astype(jnp.float32) * COST_SCALE
            costs[x + HALO, k, ny:ny + ROWS] = zero
        keep_x = jnp.logical_or(x < nx - 1, jnp.logical_not(last_x))
        for axis, keep in enumerate((keep_x, keep_y, keep_z)):
            bounds[x + HALO, axis, 0:ny] = jnp.where(keep, bound_of(abuf[axis, x]), 0.0)
            bounds[x + HALO, axis, ny:ny + ROWS] = zero
        return 0

    for c in range(4):
        for copy in copies[c]:
            copy.wait()
        lax.fori_loop(c * chunk, (c + 1) * chunk, layer, 0)

    def pack(x, _):
        for f in range(FIELDS):
            source = costs.at[x + HALO, f] if f < COSTS else bounds.at[x + HALO, f - COSTS]
            low = source[0:HALO]
            high = source[ny - HALO:ny]
            even = odd == 0
            y0[x, HALO * f:HALO * (f + 1)] = jnp.where(even, high, low)
            y1[x, HALO * f:HALO * (f + 1)] = jnp.where(even, low, high)
        return 0

    lax.fori_loop(0, nx, pack, 0)


def corner_kernel(nx, r0, r1, c0, c1):
    odd = lax.rem(lax.axis_index("gx"), 2)
    top = nx - (HALO - 1)
    for c, start in ((c0, jnp.where(odd == 0, top, 0)), (c1, jnp.where(odd == 0, 0, top))):
        for side, r in enumerate((r0, r1)):
            for d in range(HALO - 1):
                c[side, d] = r[start + d]


def put_rows(ny, costs, bounds, x, ahead, behind):
    for f in range(FIELDS):
        target = costs.at[x, f] if f < COSTS else bounds.at[x, f - COSTS]
        target[ny:ny + HALO] = ahead[HALO * f:HALO * (f + 1)]
        target[ny + ROWS - HALO:ny + ROWS] = behind[HALO * f:HALO * (f + 1)]


class Field:
    def __init__(self, tiles, costs, bounds, lifted, primal, dual_x, dual_y, dual_z):
        self.tiles = tiles
        self.costs, self.bounds = costs, bounds
        self.lifted, self.primal = lifted, primal
        self.dual_x, self.dual_y, self.dual_z = dual_x, dual_y, dual_z

    def rows(self, j):
        return pl.ds(j, ROWS, stride=self.tiles)

    def begin(self, x):
        for j in range(self.tiles):
            values = [self.costs[x, k, self.rows(j)] * (-1.0 / STEP) for k in range(COSTS)]
            values.append(jnp.zeros((ROWS, LANES), jnp.float32))
            for k, v in enumerate(simplex(values)):
                self.lifted[0][x, j, k] = v

    def along_x(self, sweep, x, j, k, here, bound):
        value = self.lifted[sweep][x + 1, j, k] - here
        if sweep:
            value = value + self.dual_x[sweep - 1][x, j, k]
        return jnp.minimum(jnp.maximum(value, -bound), bound)

    def step_dual(self, sweep, dual, x, j, k, ahead, here, bound):
        value = ahead - here
        if sweep:
            value = value + dual[x, j, k]
        return jnp.minimum(jnp.maximum(value, -bound), bound)

    def only_x(self, sweep, x):
        for j in range(self.tiles):
            bound = self.bounds[x, 0, self.rows(j)]
            for k in range(LABELS):
                self.dual_x[sweep][x, j, k] = self.along_x(sweep, x, j, k, self.lifted[sweep][x, j, k], bound)

    def layer(self, sweep, x, write):
        lifted = self.lifted[sweep]
        end = self.tiles - 1
        bound = self.bounds[x, 1, self.rows(end)]
        first = [lifted[x, 0, k] for k in range(LABELS)]
        behind_y = []
        for k in range(LABELS):
            ahead = pltpu.roll(first[k], ROWS - 1, 0)
            value = self.step_dual(sweep, self.dual_y, x, end, k, ahead, lifted[x, end, k], bound)
            self.dual_y[x, end, k] = value
            behind_y.append(pltpu.roll(value, 1, 0))
        here = first
        for j in range(self.tiles):
            bound_x, bound_y, bound_z = (self.bounds[x, d, self.rows(j)] for d in range(3))
            ahead_y = [lifted[x, j + 1, k] for k in range(LABELS)] if j < end else None
            values, old = [], []
            for k in range(LABELS):
                qx = self.along_x(sweep, x, j, k, here[k], bound_x)
                self.dual_x[sweep][x, j, k] = qx
                if j < end:
                    qy = self.step_dual(sweep, self.dual_y, x, j, k, ahead_y[k], here[k], bound_y)
                    if sweep < 2:
                        self.dual_y[x, j, k] = qy
                else:
                    qy = self.dual_y[x, j, k]
                qz = self.step_dual(sweep, self.dual_z, x, j, k, pltpu.roll(here[k], LANES - 1, 1), here[k], bound_z)
                if sweep < 2:
                    self.dual_z[x, j, k] = qz
                behind = (self.dual_x[sweep][x - 1, j, k] + behind_y[k]) + pltpu.roll(qz, 1, 1)
                adjoint = behind - ((qx + qy) + qz)
                behind_y[k] = qy
                p = here[k] if sweep == 0 else self.primal[x, j, k]
                old.append(p)
                value = p - (STEP * STEP) * adjoint
                if k < COSTS:
                    value = value - self.costs[x, k, self.rows(j)]
                values.append(value)
            updated = simplex(values)
            for k in range(LABELS):
                if sweep < 2:
                    self.primal[x, j, k] = updated[k]
                    self.lifted[sweep + 1][x, j, k] = updated[k] + (updated[k] - old[k])
                else:
                    write(x, j, k, updated[k])
            here = ahead_y


def inner_kernel(nx, ny, costs_in, bounds_in, r0, r1, costs, bounds, l0, l1, l2, primal, qx1, qx2, qx3, qy, qz, out, rowed, sem):
    del costs_in, bounds_in
    tiles = ny // ROWS + 1
    field = Field(tiles, costs, bounds, (l0, l1, l2), primal, (qx1, qx2, qx3), qy, qz)
    odd = lax.rem(lax.axis_index("gy"), 2)

    def fill(ahead, behind):
        def step(x, _):
            put_rows(ny, costs, bounds, x + HALO, ahead.at[x], behind.at[x])
            return 0
        lax.fori_loop(0, nx, step, 0)

    @pl.when(odd == 0)
    def _():
        fill(r0, r1)

    @pl.when(odd != 0)
    def _():
        fill(r1, r0)

    def write(x, j, k, value):
        rowed[x - HALO, k, pl.ds(j, ROWS, stride=tiles)] = value

    def begin(x, _):
        field.begin(x)
        return 0

    lax.fori_loop(HALO, HALO + nx, begin, 0)
    for sweep in range(3):
        low, high = HALO + sweep + 1, HALO + nx - sweep - 1
        field.only_x(sweep, low - 1)

        def step(x, _):
            field.layer(sweep, x, write)
            if sweep == 2:
                flush(rowed, out, ny, sem, x - HALO).start()
            return 0

        lax.fori_loop(low, high, step, 0)

    def finish(x, _):
        flush(rowed, out, ny, sem, x).wait()
        return 0

    lax.fori_loop(HALO, nx - HALO, finish, 0)


def flush(rowed, out, ny, sem, x):
    return pltpu.make_async_copy(rowed.at[x, :, 0:ny], out.at[:, x], sem.at[x])


def rim(nx, ny, x0, x1, c0, c1, costs, bounds, l0, l1, l2, primal, qx1, qx2, qx3, qy, qz, out, rowed, sem):
    tiles = ny // ROWS + 1
    field = Field(tiles, costs, bounds, (l0, l1, l2), primal, (qx1, qx2, qx3), qy, qz)
    odd_x = lax.rem(lax.axis_index("gx"), 2)
    odd_y = lax.rem(lax.axis_index("gy"), 2)
    zero = jnp.zeros((ROWS, LANES), jnp.float32)

    def fill(message, corners, base, side):
        for d in range(HALO):
            x = base + d
            for k in range(COSTS):
                costs[x, k, 0:ny] = message[d * COSTS + k]
                costs[x, k, ny:ny + ROWS] = zero
            bounds[x, 0, 0:ny] = message[HALO * COSTS + d]
            for axis in range(3):
                bounds[x, axis, ny:ny + ROWS] = zero
        far = base + (0 if side else HALO - 1)
        for axis in (1, 2):
            bounds[far, axis, 0:ny] = jnp.zeros((ny, LANES), jnp.float32)
        for d in range(HALO - 1):
            x = base + d + side
            for axis in (1, 2):
                bounds[x, axis, 0:ny] = message[HALO * (COSTS + 1) + 2 * d + axis - 1]

            @pl.when(odd_y == 0)
            def _():
                put_rows(ny, costs, bounds, x, corners.at[0, d], corners.at[1, d])

            @pl.when(odd_y != 0)
            def _():
                put_rows(ny, costs, bounds, x, corners.at[1, d], corners.at[0, d])

    @pl.when(odd_x == 0)
    def _():
        fill(x0, c0, HALO + nx, 0)
        fill(x1, c1, 0, 1)

    @pl.when(odd_x != 0)
    def _():
        fill(x1, c1, HALO + nx, 0)
        fill(x0, c0, 0, 1)

    def place(i, left, right):
        return jnp.where(i < HALO, left + i, right + i - HALO)

    def begin(i, _):
        field.begin(place(i, 0, HALO + nx))
        return 0

    lax.fori_loop(0, 2 * HALO, begin, 0)
    for sweep in range(3):
        left, right = 1 + sweep, nx + HALO - 1 - sweep
        field.only_x(sweep, left - 1)

        def step(i, _):
            x = place(i, left, right)

            def save(x, j, k, value):
                rowed[i, k, pl.ds(j, ROWS, stride=tiles)] = value

            field.layer(sweep, x, save)
            if sweep == 2:
                pltpu.make_async_copy(rowed.at[i, :, 0:ny], out.at[:, x - HALO], sem.at[i]).start()
            return 0

        lax.fori_loop(0, 2 * HALO, step, 0)

    def finish(i, _):
        x = place(i, left, right)
        pltpu.make_async_copy(rowed.at[i, :, 0:ny], out.at[:, x - HALO], sem.at[i]).wait()
        return 0

    lax.fori_loop(0, 2 * HALO, finish, 0)


def rim_entry(nx, ny, *refs):
    x0, x1, c0, c1 = refs[:4]
    outputs = refs[4 + 12:4 + 24]
    rowed, sem = refs[4 + 24:]
    rim(nx, ny, x0, x1, c0, c1, *outputs, rowed, sem)


def vmem(shape, dtype=jnp.float32):
    return pltpu.VMEM(shape, dtype)


def hbm(shape, dtype=jnp.float32):
    return jax.ShapeDtypeStruct(shape, dtype)


def body(unary, affinity):
    _, nx, ny, lanes = unary.shape
    tiles = ny // ROWS + 1
    wide = nx + 2 * HALO
    planes = HALO * (COSTS + 1) + 2 * (HALO - 1)
    DMA = pltpu.SemaphoreType.DMA

    m0, m1 = pl.pallas_call(
        functools.partial(edge_kernel, nx),
        in_specs=[HB, HB], out_specs=[VM, VM],
        out_shape=[vmem((planes, ny, lanes))] * 2,
        scratch_shapes=[
            pltpu.VMEM((2, LABELS, HALO, ny, lanes), jnp.int32),
            pltpu.VMEM((2, 3, HALO, ny, lanes), jnp.int32),
            DMA((4,)),
        ],
        compiler_params=params(), name="edge",
    )(unary, affinity)
    x0 = swap(m0, "gx", 0)
    x1 = swap(m1, "gx", 1)

    costs, bounds, y0, y1 = pl.pallas_call(
        functools.partial(main_kernel, nx, ny),
        in_specs=[HB, HB, VM], out_specs=[VM] * 4,
        out_shape=[
            vmem((wide, COSTS, ny + ROWS, lanes)),
            vmem((wide, 3, ny + ROWS, lanes)),
            vmem((nx, FIELDS * HALO, lanes)),
            vmem((nx, FIELDS * HALO, lanes)),
        ],
        scratch_shapes=[
            pltpu.VMEM(unary.shape, jnp.int32),
            pltpu.VMEM(affinity.shape, jnp.int32),
            DMA((8,)),
        ],
        compiler_params=params(), name="main",
    )(unary, affinity, m0)
    r0 = swap(y0, "gy", 0)
    r1 = swap(y1, "gy", 1)

    c0, c1 = pl.pallas_call(
        functools.partial(corner_kernel, nx),
        in_specs=[VM, VM], out_specs=[VM, VM],
        out_shape=[vmem((2, HALO - 1, FIELDS * HALO, lanes))] * 2,
        compiler_params=params(), name="corner",
    )(r0, r1)
    d0 = swap(c0, "gx", 0)
    d1 = swap(c1, "gx", 1)

    tiled = vmem((wide, tiles, LABELS, ROWS, lanes))
    state = pl.pallas_call(
        functools.partial(inner_kernel, nx, ny),
        in_specs=[VM] * 4, out_specs=[VM] * 11 + [HB],
        out_shape=[vmem(costs.shape), vmem(bounds.shape)] + [tiled] * 9 + [hbm(unary.shape)],
        input_output_aliases={0: 0, 1: 1},
        scratch_shapes=[pltpu.VMEM((nx, LABELS, ny + ROWS, lanes), jnp.float32), DMA((nx,))],
        compiler_params=params(), name="inner",
    )(costs, bounds, r0, r1)

    result = pl.pallas_call(
        functools.partial(rim_entry, nx, ny),
        in_specs=[VM] * 4 + [VM] * 11 + [HB], out_specs=[VM] * 11 + [HB],
        out_shape=[vmem(costs.shape), vmem(bounds.shape)] + [tiled] * 9 + [hbm(unary.shape)],
        input_output_aliases={4 + i: i for i in range(12)},
        scratch_shapes=[pltpu.VMEM((2 * HALO, LABELS, ny + ROWS, lanes), jnp.float32), DMA((2 * HALO,))],
        compiler_params=params(), name="rim",
    )(x0, x1, d0, d1, *state)
    return result[-1]


def solution(mesh):
    placed = P(None, ("slab", "gx"), "gy", None)
    return jax.shard_map(body, mesh=mesh, in_specs=(placed, placed), out_specs=placed, check_vma=False)
```

time: 82.2 us -> 37.9 us (0.46); the launches traced: 80.6 us -> 37.7 us
  other arithmetic: 30.1 us -> 0 us
  starting transfers between devices: 31.6 us -> 11.2 us
  Pallas kernels: 0 us -> 18.8 us
  local copies, waits for them, and re-layouts: 12.8 us -> 2.72 us
    ppermute x12 -> x6, starting transfers between devices: 31.6 us -> 11.2 us  [swap(): return lax.ppermute(value, axis, matching(lax.axis_size(axis), first))]
    pallas_call x0 -> x5, Pallas kernels: none -> 18.8 us  [the longest x1 11.3 us: body(): pl.pallas_call(functools.partial(inner_kernel, nx, ny), in_specs=[VM] * 4...]
    sub x12 -> x0, other arithmetic: 13.9 us -> none  [the longest x3 7.22 us: body(): updated = simplex(primal - step_size * (adjoint + label_costs))]
    min x7 -> x0, other arithmetic: 12.3 us -> none  [the longest x3 9.75 us: body(): dual_y = jnp.clip(dual_y + step_size * diff_y, -bounds[1], bounds[1])]
    slice x21 -> x0, local copies, waits for them, and re-layouts: 11 us -> none  [the longest x3 4.42 us: body(): ahead_x = jnp.concatenate([lifted[:, 1:], border_x], axis=1)]
    max x2 -> x0, other arithmetic: 1.94 us -> none  [simplex(): return jnp.maximum(values - threshold, 0.0)]
    neg x1 -> x0, other arithmetic: 1.84 us -> none  [body(): primal = simplex(-label_costs)]
    unnamed x24 -> x4, local copies, waits for them, and re-layouts: 1.85 us -> 2.72 us
  transfers between devices with their start and end apart: 12 -> 6, of which waited for: 5 -> 1; matrix products, arithmetic and copies ran while one was open for 20% -> 0% of each run, Pallas kernels for 0% -> 33%
where the time goes in v1:
time: 37.9 us; the launch traced here: 37.7 us
  Pallas kernels  18.8 us (50%)
  starting transfers between devices  11.2 us (30%)
  waiting for transfers between devices  4.95 us (13%)
  local copies, waits for them, and re-layouts  2.72 us (7%)
    pallas_call x1, Pallas kernels, body(): pl.pallas_call(functools.partial(inner_kernel, nx, ny), in_specs=[VM] * 4...  11.3 us
    ppermute x6, starting transfers between devices, swap(): return lax.ppermute(value, axis, matching(lax.axis_size(axis), first))  11.2 us
    pallas_call x1, Pallas kernels, body(): pl.pallas_call(functools.partial(rim_entry, nx, ny), in_specs=[VM] * 4 +...  5.92 us
    ppermute x6, waiting for transfers between devices, swap(): return lax.ppermute(value, axis, matching(lax.axis_size(axis), first))  4.95 us
    unnamed x4, local copies, waits for them, and re-layouts  2.72 us
    pallas_call x1, Pallas kernels, body(): pl.pallas_call(functools.partial(main_kernel, nx, ny), in_specs=[HB, HB,...  1.19 us
  transfers between devices with their start and end apart: 6, of which 1 were waited for; matrix products, arithmetic and copies ran while one was open for 0% of the time, Pallas kernels for 33%

profile of v1, /device:TPU:9, one launch (start us, length us, event | category | flops | bytes accessed | tf_op | source)
XLA Modules:
  0.0 37.7 jit_solution(7271613305321536946)
XLA Ops:
  0.0 0.0 copy-start
  0.0 1.6 %copy-done = s32[8,16,32,128]{3,2,1,0:T(8,128)S(1)} copy-done((s32[8,16,32,128]{3,2,1,0:T(8,128)S(1)}, s32[8,16,32,128]{3,2,1,0:T(8,128)}, u32[]{:S(2)}) %copy-start) | copy-done | bytes 2097176
  1.6 0.0 copy-start.1
  1.6 1.1 %copy-done.1 = s32[3,16,32,128]{3,2,1,0:T(8,128)S(1)} copy-done((s32[3,16,32,128]{3,2,1,0:T(8,128)S(1)}, s32[3,16,32,128]{3,2,1,0:T(8,128)}, u32[]{:S(2)}) %copy-start.1) | copy-done | bytes 786456
  2.7 0.4 edge.1
  3.1 3.2 %collective-permute-start.1 = (f32[28,32,128]{2,1,0:T(8,128)S(1)}, f32[28,32,128]{2,1,0:T(8,128)S(1)}, u32[]{:S(2)}, u32[]{:S(2)}) collective-permute-start(f32[28,32,128]{2,1,0:T(8,128)S(1)} %get-tuple-element.27), channel_id=1, source_target_pairs={{4,8},{8,4},{5,9},{9,5},{6,10},{10,6},{7,11},{11,7},{20,24},{24,20... | collective-permute-start | bytes 1376264 | tf_op jit(solution)/shard_map/ppermute | solution.py:44
  6.3 0.1 collective-permute-start
  6.4 1.2 %main.1 = (f32[22,7,40,128]{3,2,1,0:T(8,128)S(1)}, f32[22,3,40,128]{3,2,1,0:T(8,128)S(1)}, f32[16,30,128]{2,1,0:T(8,128)S(1)}, f32[16,30,128]{2,1,0:T(8,128)S(1)}) custom-call(s32[8,16,32,128]{3,2,1,0:T(8,128)S(1)} %copy-done, s32[3,16,32,128]{3,2,1,0:T(8,128)S(1)} %copy-done.1, f32[28,32,128]{2,1,0:T(8,128)S(1)} %get-tuple-element.26.after), custom_call_target="tpu_custom_call" | custom-call | tf_op jit(solution)/shard_map/main/pallas_call | solution.py:401
  7.6 1.0 %collective-permute-start.2 = (f32[16,30,128]{2,1,0:T(8,128)S(1)}, f32[16,30,128]{2,1,0:T(8,128)S(1)}, u32[]{:S(2)}, u32[]{:S(2)}) collective-permute-start(f32[16,30,128]{2,1,0:T(8,128)S(1)} %get-tuple-element.28), channel_id=1, source_target_pairs={{0,1},{1,0},{2,3},{3,2},{4,5},{5,4},{6,7},{7,6},{8,9},{9,8},{10,11... | collective-permute-start | bytes 737288 | tf_op jit(solution)/shard_map/ppermute | solution.py:44
  8.6 3.0 %collective-permute-start.3 = (f32[16,30,128]{2,1,0:T(8,128)S(1)}, f32[16,30,128]{2,1,0:T(8,128)S(1)}, u32[]{:S(2)}, u32[]{:S(2)}) collective-permute-start(f32[16,30,128]{2,1,0:T(8,128)S(1)} %get-tuple-element.29), channel_id=1, source_target_pairs={{1,2},{2,1},{5,6},{6,5},{9,10},{10,9},{13,14},{14,13},{17,18},{18,... | collective-permute-start | bytes 737288 | tf_op jit(solution)/shard_map/ppermute | solution.py:44
  11.6 0.0 collective-permute-done.2.r0
  11.6 4.9 %collective-permute-done.3.r1 = f32[16,30,128]{2,1,0:T(8,128)S(1)} collective-permute-done((f32[16,30,128]{2,1,0:T(8,128)S(1)}, f32[16,30,128]{2,1,0:T(8,128)S(1)}, u32[]{:S(2)}, u32[]{:S(2)}) %collective-permute-start.3) | collective-permute-done | bytes 245792 | tf_op jit(solution)/shard_map/ppermute | solution.py:44
  16.6 1.8 %collective-permute-start.4 = (f32[2,2,30,128]{3,2,1,0:T(8,128)S(1)}, f32[2,2,30,128]{3,2,1,0:T(8,128)S(1)}, u32[]{:S(2)}, u32[]{:S(2)}) collective-permute-start(f32[2,2,30,128]{3,2,1,0:T(8,128)S(1)} %get-tuple-element.30), channel_id=1, source_target_pairs={{0,4},{4,0},{8,12},{12,8},{1,5},{5,1},{9,13},{13,9},{2,6},{6,2},{1... | collective-permute-start | bytes 184328 | tf_op jit(solution)/shard_map/ppermute | solution.py:44
  18.4 2.1 %collective-permute-start.5 = (f32[2,2,30,128]{3,2,1,0:T(8,128)S(1)}, f32[2,2,30,128]{3,2,1,0:T(8,128)S(1)}, u32[]{:S(2)}, u32[]{:S(2)}) collective-permute-start(f32[2,2,30,128]{3,2,1,0:T(8,128)S(1)} %get-tuple-element.31), channel_id=1, source_target_pairs={{4,8},{8,4},{5,9},{9,5},{6,10},{10,6},{7,11},{11,7},{20,24},{24,20... | collective-permute-start | bytes 184328 | tf_op jit(solution)/shard_map/ppermute | solution.py:44
  20.5 11.3 %inner.1 = (f32[22,7,40,128]{3,2,1,0:T(8,128)S(1)}, f32[22,3,40,128]{3,2,1,0:T(8,128)S(1)}, f32[22,5,8,8,128]{4,3,2,1,0:T(8,128)S(1)}, f32[22,5,8,8,128]{4,3,2,1...) custom-call(f32[22,7,40,128]{3,2,1,0:T(8,128)S(1)} %get-tuple-elemen, ...), custom_call_target="tpu_custom_call", output_to_operand_aliasing={{0}: (0, {}), {1}: (1, {})} | custom-call | tf_op jit(solution)/shard_map/inner/pallas_call | solution.py:430
  31.8 0.0 collective-permute-done.4.refs_2_
  31.8 0.0 collective-permute-done.5.refs_3_
  31.8 0.0 collective-permute-done.1.refs_1_
  31.8 0.0 collective-permute-done.refs_0_
  31.8 5.9 %rim.1 = (f32[22,7,40,128]{3,2,1,0:T(8,128)S(1)}, f32[22,3,40,128]{3,2,1,0:T(8,128)S(1)}, f32[22,5,8,8,128]{4,3,2,1,0:T(8,128)S(1)}, f32[22,5,8,8,128]{4,3,2,1,0...) custom-call(f32[28,32,128]{2,1,0:T(8,128)S(1)} %collective-permute-d, ...), custom_call_target="tpu_custom_call", output_to_operand_aliasing={{0}: (4, {}), {1}: (5, {}), {2}: (6, {}), {3}: (7, {}), {4}... | custom-call | tf_op jit(solution)/shard_map/rim/pallas_call | solution.py:439
  (1 shorter events, 0.0 us)
Async XLA Ops:
  0.0 1.6 %copy-start = (s32[8,16,32,128]{3,2,1,0:T(8,128)S(1)}, s32[8,16,32,128]{3,2,1,0:T(8,128)}, u32[]{:S(2)}) copy-start(s32[8,16,32,128]{3,2,1,0:T(8,128)} %u_hbm.3) | copy-start | bytes 6291460
  1.6 1.1 %copy-start.1 = (s32[3,16,32,128]{3,2,1,0:T(8,128)S(1)}, s32[3,16,32,128]{3,2,1,0:T(8,128)}, u32[]{:S(2)}) copy-start(s32[3,16,32,128]{3,2,1,0:T(8,128)} %a_hbm.3) | copy-start | bytes 2359300
  3.1 28.7 %collective-permute-start.1 = (f32[28,32,128]{2,1,0:T(8,128)S(1)}, f32[28,32,128]{2,1,0:T(8,128)S(1)}, u32[]{:S(2)}, u32[]{:S(2)}) collective-permute-start(f32[28,32,128]{2,1,0:T(8,128)S(1)} %get-tuple-element.27), channel_id=1, source_target_pairs={{4,8},{8,4},{5,9},{9,5},{6,10},{10,6},{7,11},{11,7},{20,24},{24,20... | collective-permute-start | bytes 1376264 | tf_op jit(solution)/shard_map/ppermute | solution.py:44
  6.3 25.5 %collective-permute-start = (f32[28,32,128]{2,1,0:T(8,128)S(1)}, f32[28,32,128]{2,1,0:T(8,128)S(1)}, u32[]{:S(2)}, u32[]{:S(2)}) collective-permute-start(f32[28,32,128]{2,1,0:T(8,128)S(1)} %get-tuple-element.26.after), channel_id=1, source_target_pairs={{0,4},{4,0},{8,12},{12,8},{1,5},{5,1},{9,13},{13,9},{2,6},{6,2},{1... | collective-permute-start | bytes 1376264 | tf_op jit(solution)/shard_map/ppermute | solution.py:44
  7.6 4.0 %collective-permute-start.2 = (f32[16,30,128]{2,1,0:T(8,128)S(1)}, f32[16,30,128]{2,1,0:T(8,128)S(1)}, u32[]{:S(2)}, u32[]{:S(2)}) collective-permute-start(f32[16,30,128]{2,1,0:T(8,128)S(1)} %get-tuple-element.28), channel_id=1, source_target_pairs={{0,1},{1,0},{2,3},{3,2},{4,5},{5,4},{6,7},{7,6},{8,9},{9,8},{10,11... | collective-permute-start | bytes 737288 | tf_op jit(solution)/shard_map/ppermute | solution.py:44
  8.6 8.0 %collective-permute-start.3 = (f32[16,30,128]{2,1,0:T(8,128)S(1)}, f32[16,30,128]{2,1,0:T(8,128)S(1)}, u32[]{:S(2)}, u32[]{:S(2)}) collective-permute-start(f32[16,30,128]{2,1,0:T(8,128)S(1)} %get-tuple-element.29), channel_id=1, source_target_pairs={{1,2},{2,1},{5,6},{6,5},{9,10},{10,9},{13,14},{14,13},{17,18},{18,... | collective-permute-start | bytes 737288 | tf_op jit(solution)/shard_map/ppermute | solution.py:44
  16.6 15.2 %collective-permute-start.4 = (f32[2,2,30,128]{3,2,1,0:T(8,128)S(1)}, f32[2,2,30,128]{3,2,1,0:T(8,128)S(1)}, u32[]{:S(2)}, u32[]{:S(2)}) collective-permute-start(f32[2,2,30,128]{3,2,1,0:T(8,128)S(1)} %get-tuple-element.30), channel_id=1, source_target_pairs={{0,4},{4,0},{8,12},{12,8},{1,5},{5,1},{9,13},{13,9},{2,6},{6,2},{1... | collective-permute-start | bytes 184328 | tf_op jit(solution)/shard_map/ppermute | solution.py:44
  18.4 13.4 %collective-permute-start.5 = (f32[2,2,30,128]{3,2,1,0:T(8,128)S(1)}, f32[2,2,30,128]{3,2,1,0:T(8,128)S(1)}, u32[]{:S(2)}, u32[]{:S(2)}) collective-permute-start(f32[2,2,30,128]{3,2,1,0:T(8,128)S(1)} %get-tuple-element.31), channel_id=1, source_target_pairs={{4,8},{8,4},{5,9},{9,5},{6,10},{10,6},{7,11},{11,7},{20,24},{24,20... | collective-permute-start | bytes 184328 | tf_op jit(solution)/shard_map/ppermute | solution.py:44

commit v2 on v1

v2 whole, which is shorter than its diff:
```python
import functools

import jax
import jax.numpy as jnp
from jax import lax
from jax.experimental import pallas as pl
from jax.experimental.pallas import tpu as pltpu
from jax.sharding import PartitionSpec as P

STEP = 0.28
LABELS = 8
COSTS = LABELS - 1
FIELDS = COSTS + 3
HALO = 3
ROWS = 8
LANES = 128
COST_SCALE = STEP / 64.0
CHUNKS = 4

NETWORK = [
    (0, 1), (2, 3), (4, 5), (6, 7),
    (0, 2), (1, 3), (4, 6), (5, 7),
    (1, 2), (5, 6),
    (0, 4), (1, 5), (2, 6), (3, 7),
    (2, 4), (3, 5),
    (1, 2), (3, 4), (5, 6),
]

VM = pl.BlockSpec(memory_space=pltpu.VMEM)
HB = pl.BlockSpec(memory_space=pltpu.HBM)
DMA = pltpu.SemaphoreType.DMA


def params(mebibytes=6):
    return pltpu.CompilerParams(vmem_limit_bytes=mebibytes << 20)


def work(flops):
    return pl.CostEstimate(flops=flops, bytes_accessed=0, transcendentals=0)


def matching(count, first):
    pairs = []
    for low in range(first, count - 1, 2):
        pairs += [(low, low + 1), (low + 1, low)]
    return pairs


def swap(value, axis, first):
    return lax.ppermute(value, axis, matching(lax.axis_size(axis), first))


def simplex(values):
    s = list(values)
    for a, b in NETWORK:
        s[a], s[b] = jnp.maximum(s[a], s[b]), jnp.minimum(s[a], s[b])
    running = s[0] - 1.0
    threshold = running
    for k in range(1, len(s)):
        running = running + s[k]
        threshold = jnp.maximum(threshold, running * (1.0 / (k + 1)))
    return [jnp.maximum(v - threshold, 0.0) for v in values]


def bound_of(levels):
    return (0.5 / STEP) * (0.05 + 0.95 / 255.0 * levels.astype(jnp.float32))


def load_kernel(nx, ny, u_hbm, a_hbm, costs, bounds, y0, y1, ubuf, abuf, sems):
    chunk = nx // CHUNKS
    copies = []
    for c in range(CHUNKS):
        part = pl.ds(c * chunk, chunk)
        copies.append((
            pltpu.make_async_copy(u_hbm.at[:, part], ubuf.at[:, part], sems.at[2 * c]),
            pltpu.make_async_copy(a_hbm.at[:, part], abuf.at[:, part], sems.at[2 * c + 1]),
        ))
    for pair in copies:
        for c in pair:
            c.start()
    last_x = lax.axis_index("gx") == lax.axis_size("gx") - 1
    last_y = lax.axis_index("gy") == lax.axis_size("gy") - 1
    odd_y = lax.rem(lax.axis_index("gy"), 2)
    row = lax.broadcasted_iota(jnp.int32, (ny, LANES), 0)
    lane = lax.broadcasted_iota(jnp.int32, (ny, LANES), 1)
    keep_y = jnp.logical_or(row < ny - 1, jnp.logical_not(last_y))
    keep_z = lane < LANES - 1
    zero = jnp.zeros((ROWS, LANES), jnp.float32)

    def layer(x, _):
        last = ubuf[LABELS - 1, x]
        for k in range(COSTS):
            costs[x + HALO, k, 0:ny] = (ubuf[k, x] - last).astype(jnp.float32) * COST_SCALE
            costs[x + HALO, k, ny:ny + ROWS] = zero
        keep_x = jnp.logical_or(x < nx - 1, jnp.logical_not(last_x))
        for axis, keep in enumerate((keep_x, keep_y, keep_z)):
            bounds[x + HALO, axis, 0:ny] = jnp.where(keep, bound_of(abuf[axis, x]), 0.0)
            bounds[x + HALO, axis, ny:ny + ROWS] = zero
        even = odd_y == 0
        for f in range(FIELDS):
            source = costs.at[x + HALO, f] if f < COSTS else bounds.at[x + HALO, f - COSTS]
            low = source[0:HALO]
            high = source[ny - HALO:ny]
            y0[x, HALO * f:HALO * (f + 1)] = jnp.where(even, high, low)
            y1[x, HALO * f:HALO * (f + 1)] = jnp.where(even, low, high)
        return 0

    for c in range(CHUNKS):
        for copy in copies[c]:
            copy.wait()
        lax.fori_loop(c * chunk, (c + 1) * chunk, layer, 0)


def edge_kernel(nx, ny, costs, bounds, m0, m1):
    odd_x = lax.rem(lax.axis_index("gx"), 2)
    for m, side in ((m0, 1 - odd_x), (m1, odd_x)):
        start = HALO + side * (nx - HALO)
        for d in range(HALO):
            for k in range(COSTS):
                m[d * COSTS + k] = costs[start + d, k, 0:ny]
            m[HALO * COSTS + d] = bounds[start + d, 0, 0:ny]
        for d in range(HALO - 1):
            for axis in (1, 2):
                m[HALO * (COSTS + 1) + 2 * d + axis - 1] = bounds[start + d + side, axis, 0:ny]


def corner_kernel(nx, r0, r1, mark, c0, c1):
    del mark
    odd = lax.rem(lax.axis_index("gx"), 2)
    top = nx - (HALO - 1)
    for c, start in ((c0, jnp.where(odd == 0, top, 0)), (c1, jnp.where(odd == 0, 0, top))):
        for side, r in enumerate((r0, r1)):
            for d in range(HALO - 1):
                c[side, d] = r[start + d]


def put_rows(ny, costs, bounds, x, ahead, behind):
    for f in range(FIELDS):
        target = costs.at[x, f] if f < COSTS else bounds.at[x, f - COSTS]
        target[ny:ny + HALO] = ahead[HALO * f:HALO * (f + 1)]
        target[ny + ROWS - HALO:ny + ROWS] = behind[HALO * f:HALO * (f + 1)]


class Field:
    def __init__(self, tiles, scratch, costs, bounds, l0, l1, l2, primal, qx1, qx2, qx3, qy, qz):
        self.tiles = tiles
        self.slope_z, self.held = scratch
        self.costs, self.bounds = costs, bounds
        self.lifted, self.primal = (l0, l1, l2), primal
        self.dual_x, self.dual_y, self.dual_z = (qx1, qx2, qx3), qy, qz

    def at(self, t, offset=0):
        return pl.ds(ROWS * t + offset, ROWS)

    def put_lifted(self, sweep, x, t, k, value):
        self.lifted[sweep][x, k, self.at(t)] = value
        if t == 0:
            self.lifted[sweep][x, k, self.at(self.tiles)] = value

    def begin(self, x, tiles):
        for t in tiles:
            values = [self.costs[x, k, self.at(t)] * (-1.0 / STEP) for k in range(COSTS)]
            values.append(jnp.zeros((ROWS, LANES), jnp.float32))
            for k, v in enumerate(simplex(values)):
                self.put_lifted(0, x, t, k, v)

    def clipped(self, sweep, old, slope, bound):
        value = slope if sweep == 0 else old() + slope
        return jnp.minimum(jnp.maximum(value, -bound), bound)

    def turn(self, sweep, x, tiles):
        for t in tiles:
            for k in range(LABELS):
                here = self.lifted[sweep][x, k, self.at(t)]
                self.slope_z[k, self.at(t)] = pltpu.roll(here, LANES - 1, 1) - here

    def one_x(self, sweep, x, t, k, here, bound):
        slope = self.lifted[sweep][x + 1, k, self.at(t)] - here
        value = self.clipped(sweep, lambda: self.dual_x[sweep - 1][x, k, self.at(t)], slope, bound)
        self.dual_x[sweep][x, k, self.at(t)] = value
        return value

    def one_y(self, sweep, x, t, k, here, bound):
        slope = self.lifted[sweep][x, k, self.at(t, 1)] - here
        value = self.clipped(sweep, lambda: self.dual_y[x, k, self.at(t + 1)], slope, bound)
        self.dual_y[x, k, self.at(t + 1)] = value
        if t == self.tiles - 1:
            self.dual_y[x, k, self.at(0)] = value
        return value

    def one_z(self, sweep, x, t, k, bound):
        value = self.clipped(sweep, lambda: self.dual_z[x, k, self.at(t)], self.slope_z[k, self.at(t)], bound)
        if sweep < 2:
            self.dual_z[x, k, self.at(t)] = value
        return value

    def step_x(self, sweep, x, t):
        bound = self.bounds[x, 0, self.at(t)]
        for k in range(LABELS):
            self.one_x(sweep, x, t, k, self.lifted[sweep][x, k, self.at(t)], bound)

    def step_y(self, sweep, x, t):
        bound = self.bounds[x, 1, self.at(t)]
        for k in range(LABELS):
            self.one_y(sweep, x, t, k, self.lifted[sweep][x, k, self.at(t)], bound)

    def duals(self, sweep, x, tiles, extra):
        for t in extra:
            self.step_y(sweep, x, t)
        order = sorted(tiles, key=lambda t: (t + 1) % self.tiles)
        for t in order:
            bounds = [self.bounds[x, d, self.at(t)] for d in range(3)]
            for k in range(LABELS):
                here = self.lifted[sweep][x, k, self.at(t)]
                qz = self.one_z(sweep, x, t, k, bounds[2])
                qx = self.one_x(sweep, x, t, k, here, bounds[0])
                qy = self.one_y(sweep, x, t, k, here, bounds[1])
                later = t == self.tiles - 1 and t - 1 in tiles
                behind = self.dual_x[sweep][x - 1, k, self.at(t)] + pltpu.roll(qz, 1, 1)
                if not later:
                    behind = behind + self.dual_y[x, k, self.at(t, ROWS - 1)]
                self.held[k, self.at(t)] = ((qx + qy) + qz) - behind
        if self.tiles - 1 in tiles and self.tiles - 2 in tiles:
            t = self.tiles - 1
            for k in range(LABELS):
                self.held[k, self.at(t)] = self.held[k, self.at(t)] - self.dual_y[x, k, self.at(t, ROWS - 1)]

    def project(self, sweep, x, tiles, write):
        for t in tiles:
            primal = self.lifted[0] if sweep == 0 else self.primal
            old = [primal[x, k, self.at(t)] for k in range(LABELS)]
            values = []
            for k in range(LABELS):
                change = self.held[k, self.at(t)] * (STEP * STEP)
                if k < COSTS:
                    change = change - self.costs[x, k, self.at(t)]
                values.append(old[k] + change)
            updated = simplex(values)
            for k in range(LABELS):
                if sweep < 2:
                    self.primal[x, k, self.at(t)] = updated[k]
                    self.put_lifted(sweep + 1, x, t, k, updated[k] + (updated[k] - old[k]))
                else:
                    write(k, self.at(t), updated[k])

    def sweep(self, sweep, count, place, tiles, extra=(), write=None, written=None):
        def project(i):
            self.project(sweep, place(i), tiles, None if write is None else functools.partial(write, i))
            if written is not None:
                written(i)

        def step(i, _):
            project(i - 1)
            self.duals(sweep, place(i), tiles, extra)
            self.turn(sweep, place(i + 1), tiles)
            return 0

        self.turn(sweep, place(0), tiles)
        self.duals(sweep, place(0), tiles, extra)
        self.turn(sweep, place(1), tiles)
        lax.fori_loop(1, count, step, 0)
        project(count - 1)


def scratch_fields(rows, lanes):
    return [pltpu.VMEM((LABELS, rows, lanes), jnp.float32)] * 2


STATE = 11


def start_kernel(nx, ny, *refs):
    state, mark, scratch = refs[2:2 + STATE], refs[2 + STATE], refs[3 + STATE:]
    mark[...] = jnp.zeros_like(mark)
    tiles = ny // ROWS + 1
    field = Field(tiles, scratch, *state)

    def begin(x, _):
        field.begin(x, range(tiles - 1))
        return 0

    lax.fori_loop(HALO, HALO + nx, begin, 0)
    inner = range(1, tiles - 2)
    for t in inner:
        field.step_x(0, HALO, t)
    field.sweep(0, nx - 2, lambda i: HALO + 1 + i, inner, extra=(0,))


def inner_kernel(nx, ny, *refs):
    r0, r1 = refs[:2]
    state = refs[2 + STATE:2 + 2 * STATE]
    out, *scratch, rowed, sem = refs[2 + 2 * STATE:]
    costs, bounds = state[:2]
    tiles = ny // ROWS + 1
    everything = range(tiles)
    field = Field(tiles, scratch, *state)
    odd = lax.rem(lax.axis_index("gy"), 2)

    def fill(ahead, behind):
        def step(x, _):
            put_rows(ny, costs, bounds, x + HALO, ahead.at[x], behind.at[x])
            return 0
        lax.fori_loop(0, nx, step, 0)

    @pl.when(odd == 0)
    def _():
        fill(r0, r1)

    @pl.when(odd != 0)
    def _():
        fill(r1, r0)

    def begin(x, _):
        field.begin(x, [tiles - 1])
        return 0

    lax.fori_loop(HALO, HALO + nx, begin, 0)
    outer = [0, tiles - 2, tiles - 1]
    for t in outer:
        field.step_x(0, HALO, t)
    field.sweep(0, nx - 2, lambda i: HALO + 1 + i, outer)
    for t in everything:
        field.step_x(1, HALO + 1, t)
    field.sweep(1, nx - 4, lambda i: HALO + 2 + i, everything)
    for t in range(tiles - 1):
        field.step_x(2, HALO + 2, t)

    def write(i, k, rows, value):
        rowed[i, k, rows] = value

    def flush(i):
        return pltpu.make_async_copy(rowed.at[i], out.at[:, i + HALO], sem.at[i])

    field.sweep(2, nx - 6, lambda i: HALO + 3 + i, range(tiles - 1), (tiles - 1,), write, lambda i: flush(i).start())

    def finish(i, _):
        flush(i).wait()
        return 0

    lax.fori_loop(0, nx - 6, finish, 0)


def rim_kernel(nx, ny, *refs):
    x0, x1, c0, c1 = refs[:4]
    state = refs[4 + STATE + 1:4 + STATE + 1 + STATE]
    out, *scratch, rowed, sem = refs[4 + STATE + 1 + STATE:]
    costs, bounds = state[:2]
    tiles = ny // ROWS + 1
    everything = range(tiles)
    field = Field(tiles, scratch, *state)
    odd_x = lax.rem(lax.axis_index("gx"), 2)
    odd_y = lax.rem(lax.axis_index("gy"), 2)
    zero = jnp.zeros((ROWS, LANES), jnp.float32)

    def fill(message, corners, base, side):
        for d in range(HALO):
            x = base + d
            for k in range(COSTS):
                costs[x, k, 0:ny] = message[d * COSTS + k]
                costs[x, k, ny:ny + ROWS] = zero
            bounds[x, 0, 0:ny] = message[HALO * COSTS + d]
            for axis in range(3):
                bounds[x, axis, ny:ny + ROWS] = zero
        far = base + (0 if side else HALO - 1)
        for axis in (1, 2):
            bounds[far, axis, 0:ny] = jnp.zeros((ny, LANES), jnp.float32)
        for d in range(HALO - 1):
            x = base + d + side
            for axis in (1, 2):
                bounds[x, axis, 0:ny] = message[HALO * (COSTS + 1) + 2 * d + axis - 1]

            @pl.when(odd_y == 0)
            def _():
                put_rows(ny, costs, bounds, x, corners.at[0, d], corners.at[1, d])

            @pl.when(odd_y != 0)
            def _():
                put_rows(ny, costs, bounds, x, corners.at[1, d], corners.at[0, d])

    @pl.when(odd_x == 0)
    def _():
        fill(x0, c0, HALO + nx, 0)
        fill(x1, c1, 0, 1)

    @pl.when(odd_x != 0)
    def _():
        fill(x1, c1, HALO + nx, 0)
        fill(x0, c0, 0, 1)

    def place(i, left, right):
        return jnp.where(i < HALO, left + i, right + i - HALO)

    def begin(i, _):
        field.begin(place(i, 0, HALO + nx), everything)
        return 0

    lax.fori_loop(0, 2 * HALO, begin, 0)

    def write(i, k, rows, value):
        rowed[i, k, rows] = value

    def flush(i):
        return pltpu.make_async_copy(rowed.at[i], out.at[:, place(i, 0, nx - HALO)], sem.at[i])

    for sweep in range(3):
        at = functools.partial(place, left=1 + sweep, right=nx + HALO - 1 - sweep)
        used = everything if sweep < 2 else range(tiles - 1)
        for t in used:
            field.step_x(sweep, sweep, t)
        if sweep < 2:
            field.sweep(sweep, 2 * HALO, at, used)
        else:
            field.sweep(sweep, 2 * HALO, at, used, (tiles - 1,), write, lambda i: flush(i).start())

    def finish(i, _):
        flush(i).wait()
        return 0

    lax.fori_loop(0, 2 * HALO, finish, 0)


def vmem(*shape):
    return pltpu.VMEM(shape, jnp.float32)


def body(unary, affinity):
    _, nx, ny, lanes = unary.shape
    full = ny + ROWS
    wide = nx + 2 * HALO
    planes = HALO * (COSTS + 1) + 2 * (HALO - 1)
    costs_shape, bounds_shape = vmem(wide, COSTS, full, lanes), vmem(wide, 3, full, lanes)
    edge_shape, row_shape = vmem(planes, ny, lanes), vmem(nx, FIELDS * HALO, lanes)

    costs, bounds, y0, y1 = pl.pallas_call(
        functools.partial(load_kernel, nx, ny),
        in_specs=[HB, HB], out_specs=[VM] * 4,
        out_shape=[costs_shape, bounds_shape, row_shape, row_shape],
        scratch_shapes=[pltpu.VMEM(unary.shape, jnp.int32), pltpu.VMEM(affinity.shape, jnp.int32), DMA((2 * CHUNKS,))],
        compiler_params=params(54), cost_estimate=work(1), name="load",
    )(unary, affinity)
    r1 = swap(y1, "gy", 1)
    r0 = swap(y0, "gy", 0)
    m0, m1 = pl.pallas_call(
        functools.partial(edge_kernel, nx, ny),
        in_specs=[VM] * 2, out_specs=[VM] * 2, out_shape=[edge_shape] * 2,
        compiler_params=params(), cost_estimate=work(1), name="edge",
    )(costs, bounds)
    x0 = swap(m0, "gx", 0)
    x1 = swap(m1, "gx", 1)

    padded, plain = vmem(wide, LABELS, full + 2 * ROWS, lanes), vmem(wide, LABELS, full, lanes)
    shapes = [costs_shape, bounds_shape, padded, padded, padded, plain, plain, plain, plain, padded, plain]
    scratch = scratch_fields(full, lanes)
    result = jax.ShapeDtypeStruct(unary.shape, jnp.float32)

    *state, mark = pl.pallas_call(
        functools.partial(start_kernel, nx, ny),
        in_specs=[VM] * 2, out_specs=[VM] * (STATE + 1), out_shape=shapes + [vmem(ROWS, lanes)],
        input_output_aliases={0: 0, 1: 1},
        scratch_shapes=scratch,
        compiler_params=params(), cost_estimate=work(1), name="start",
    )(costs, bounds)

    c0, c1 = pl.pallas_call(
        functools.partial(corner_kernel, nx),
        in_specs=[VM] * 3, out_specs=[VM, VM],
        out_shape=[vmem(2, HALO - 1, FIELDS * HALO, lanes)] * 2,
        compiler_params=params(), cost_estimate=work(1), name="corner",
    )(r0, r1, mark)
    d0 = swap(c0, "gx", 0)
    d1 = swap(c1, "gx", 1)

    state = pl.pallas_call(
        functools.partial(inner_kernel, nx, ny),
        in_specs=[VM] * (2 + STATE), out_specs=[VM] * STATE + [HB], out_shape=shapes + [result],
        input_output_aliases={2 + i: i for i in range(STATE)},
        scratch_shapes=scratch + [pltpu.VMEM((nx - 2 * HALO, LABELS, ny, lanes), jnp.float32), DMA((nx - 2 * HALO,))],
        compiler_params=params(), cost_estimate=work(10**11), name="inner",
    )(r0, r1, *state)

    state = pl.pallas_call(
        functools.partial(rim_kernel, nx, ny),
        in_specs=[VM] * (4 + STATE) + [HB], out_specs=[VM] * STATE + [HB], out_shape=shapes + [result],
        input_output_aliases={4 + i: i for i in range(STATE + 1)},
        scratch_shapes=scratch + [pltpu.VMEM((2 * HALO, LABELS, ny, lanes), jnp.float32), DMA((2 * HALO,))],
        compiler_params=params(), cost_estimate=work(10**11), name="rim",
    )(x0, x1, d0, d1, *state)
    return state[-1]


def solution(mesh):
    placed = P(None, ("slab", "gx"), "gy", None)
    return jax.shard_map(body, mesh=mesh, in_specs=(placed, placed), out_specs=placed, check_vma=False)
```

time: 37.9 us -> 29.6 us (0.78)
  the two profiles are of different devices: /device:TPU:9 before, /device:TPU:1 now
where the time goes in v2:
time: 29.6 us; the launch traced here: 29.4 us
  Pallas kernels  18.1 us (61%)
  starting transfers between devices  11.2 us (38%)
    ppermute x6, starting transfers between devices, swap(): return lax.ppermute(value, axis, matching(lax.axis_size(axis), first))  11.2 us
    pallas_call x1, Pallas kernels, body(): pl.pallas_call(functools.partial(inner_kernel, nx, ny), in_specs=[VM] * (...  8.11 us
    pallas_call x1, Pallas kernels, body(): pl.pallas_call(functools.partial(rim_kernel, nx, ny), in_specs=[VM] * (4...  5.43 us
    pallas_call x1, Pallas kernels, body(): pl.pallas_call(functools.partial(start_kernel, nx, ny), in_specs=[VM] * 2...  2.55 us
    pallas_call x1, Pallas kernels, body(): pl.pallas_call(functools.partial(load_kernel, nx, ny), in_specs=[HB, HB],...  1.94 us
  transfers between devices with their start and end apart: 6, of which 0 were waited for; matrix products, arithmetic and copies ran while one was open for 0% of the time, Pallas kernels for 37%

profile of v2, /device:TPU:1, one launch (start us, length us, event | category | flops | bytes accessed | tf_op | source)
XLA Modules:
  0.0 29.4 jit_solution(12136135977458866967)
XLA Ops:
  0.0 1.9 %load.1 = (f32[22,7,40,128]{3,2,1,0:T(8,128)S(1)}, f32[22,3,40,128]{3,2,1,0:T(8,128)S(1)}, f32[16,30,128]{2,1,0:T(8,128)S(1)}, f32[16,30,128]{2,1,0:T(8,128)S(1)}) custom-call(s32[8,16,32,128]{3,2,1,0:T(8,128)} %u_hbm.1, s32[3,16,32,128]{3,2,1,0:T(8,128)} %a_hbm.1), custom_call_target="tpu_custom_call" | custom-call | flops 1 | tf_op jit(solution)/shard_map/load/pallas_call | solution.py:434
  1.9 0.1 collective-permute-start.2
  2.1 4.5 %collective-permute-start.3 = (f32[16,30,128]{2,1,0:T(8,128)S(1)}, f32[16,30,128]{2,1,0:T(8,128)S(1)}, u32[]{:S(2)}, u32[]{:S(2)}) collective-permute-start(f32[16,30,128]{2,1,0:T(8,128)S(1)} %get-tuple-element.43), channel_id=1, source_target_pairs={{1,2},{2,1},{5,6},{6,5},{9,10},{10,9},{13,14},{14,13},{17,18},{18,... | collective-permute-start | bytes 737288 | tf_op jit(solution)/shard_map/ppermute | solution.py:50
  6.5 0.1 edge.1
  6.6 1.4 %collective-permute-start = (f32[28,32,128]{2,1,0:T(8,128)S(1)}, f32[28,32,128]{2,1,0:T(8,128)S(1)}, u32[]{:S(2)}, u32[]{:S(2)}) collective-permute-start(f32[28,32,128]{2,1,0:T(8,128)S(1)} %get-tuple-element.40), channel_id=1, source_target_pairs={{0,4},{4,0},{8,12},{12,8},{1,5},{5,1},{9,13},{13,9},{2,6},{6,2},{1... | collective-permute-start | bytes 1376264 | tf_op jit(solution)/shard_map/ppermute | solution.py:50
  8.0 0.7 %collective-permute-start.1 = (f32[28,32,128]{2,1,0:T(8,128)S(1)}, f32[28,32,128]{2,1,0:T(8,128)S(1)}, u32[]{:S(2)}, u32[]{:S(2)}) collective-permute-start(f32[28,32,128]{2,1,0:T(8,128)S(1)} %get-tuple-element.41), channel_id=1, source_target_pairs={{4,8},{8,4},{5,9},{9,5},{6,10},{10,6},{7,11},{11,7},{20,24},{24,20... | collective-permute-start | bytes 1376264 | tf_op jit(solution)/shard_map/ppermute | solution.py:50
  8.7 2.6 %start.1 = (f32[22,7,40,128]{3,2,1,0:T(8,128)S(1)}, f32[22,3,40,128]{3,2,1,0:T(8,128)S(1)}, f32[22,8,56,128]{3,2,1,0:T(8,128)S(1)}, f32[22,8,56,128]{3,2,1,0:T(8...) custom-call(f32[22,7,40,128]{3,2,1,0:T(8,128)S(1)} %get-tuple-elemen, ...), custom_call_target="tpu_custom_call", output_to_operand_aliasing={{0}: (0, {}), {1}: (1, {})} | custom-call | flops 1 | tf_op jit(solution)/shard_map/start/pallas_call | solution.py:456
  11.2 0.0 collective-permute-done.2.r0.refs_0_
  11.2 0.0 collective-permute-done.3.r1.refs_1_
  11.3 3.9 %collective-permute-start.4 = (f32[2,2,30,128]{3,2,1,0:T(8,128)S(1)}, f32[2,2,30,128]{3,2,1,0:T(8,128)S(1)}, u32[]{:S(2)}, u32[]{:S(2)}) collective-permute-start(f32[2,2,30,128]{3,2,1,0:T(8,128)S(1)} %get-tuple-element.45), channel_id=1, source_target_pairs={{0,4},{4,0},{8,12},{12,8},{1,5},{5,1},{9,13},{13,9},{2,6},{6,2},{1... | collective-permute-start | bytes 184328 | tf_op jit(solution)/shard_map/ppermute | solution.py:50
  15.2 0.7 %collective-permute-start.5 = (f32[2,2,30,128]{3,2,1,0:T(8,128)S(1)}, f32[2,2,30,128]{3,2,1,0:T(8,128)S(1)}, u32[]{:S(2)}, u32[]{:S(2)}) collective-permute-start(f32[2,2,30,128]{3,2,1,0:T(8,128)S(1)} %get-tuple-element.46), channel_id=1, source_target_pairs={{4,8},{8,4},{5,9},{9,5},{6,10},{10,6},{7,11},{11,7},{20,24},{24,20... | collective-permute-start | bytes 184328 | tf_op jit(solution)/shard_map/ppermute | solution.py:50
  15.8 8.1 %inner.1 = (f32[22,7,40,128]{3,2,1,0:T(8,128)S(1)}, f32[22,3,40,128]{3,2,1,0:T(8,128)S(1)}, f32[22,8,56,128]{3,2,1,0:T(8,128)S(1)}, f32[22,8,56,128]{3,2,1,0:T(8...) custom-call(f32[16,30,128]{2,1,0:T(8,128)S(1)} %collective-permute-d, ...), custom_call_target="tpu_custom_call", output_to_operand_aliasing={{0}: (2, {}), {1}: (3, {}), {2}: (4, {}), {3}: (5, {}), {4}... | custom-call | flops 99999997952 | tf_op jit(solution)/shard_map/inner/pallas_call | solution.py:473
  23.9 0.0 collective-permute-done.4.refs_2_
  24.0 0.0 collective-permute-done.5.refs_3_
  24.0 0.0 collective-permute-done.refs_0_
  24.0 0.0 collective-permute-done.1.refs_1_
  24.0 5.4 %rim.1 = (f32[22,7,40,128]{3,2,1,0:T(8,128)S(1)}, f32[22,3,40,128]{3,2,1,0:T(8,128)S(1)}, f32[22,8,56,128]{3,2,1,0:T(8,128)S(1)}, f32[22,8,56,128]{3,2,1,0:T(8,1...) custom-call(f32[28,32,128]{2,1,0:T(8,128)S(1)} %collective-permute-d, ...), custom_call_target="tpu_custom_call", output_to_operand_aliasing={{0}: (4, {}), {1}: (5, {}), {2}: (6, {}), {3}: (7, {}), {4}... | custom-call | flops 99999997952 | tf_op jit(solution)/shard_map/rim/pallas_call | solution.py:481
  (1 shorter events, 0.0 us)
Async XLA Ops:
  1.9 9.3 %collective-permute-start.2 = (f32[16,30,128]{2,1,0:T(8,128)S(1)}, f32[16,30,128]{2,1,0:T(8,128)S(1)}, u32[]{:S(2)}, u32[]{:S(2)}) collective-permute-start(f32[16,30,128]{2,1,0:T(8,128)S(1)} %get-tuple-element.42), channel_id=1, source_target_pairs={{0,1},{1,0},{2,3},{3,2},{4,5},{5,4},{6,7},{7,6},{8,9},{9,8},{10,11... | collective-permute-start | bytes 737288 | tf_op jit(solution)/shard_map/ppermute | solution.py:50
  2.1 9.2 %collective-permute-start.3 = (f32[16,30,128]{2,1,0:T(8,128)S(1)}, f32[16,30,128]{2,1,0:T(8,128)S(1)}, u32[]{:S(2)}, u32[]{:S(2)}) collective-permute-start(f32[16,30,128]{2,1,0:T(8,128)S(1)} %get-tuple-element.43), channel_id=1, source_target_pairs={{1,2},{2,1},{5,6},{6,5},{9,10},{10,9},{13,14},{14,13},{17,18},{18,... | collective-permute-start | bytes 737288 | tf_op jit(solution)/shard_map/ppermute | solution.py:50
  6.6 17.3 %collective-permute-start = (f32[28,32,128]{2,1,0:T(8,128)S(1)}, f32[28,32,128]{2,1,0:T(8,128)S(1)}, u32[]{:S(2)}, u32[]{:S(2)}) collective-permute-start(f32[28,32,128]{2,1,0:T(8,128)S(1)} %get-tuple-element.40), channel_id=1, source_target_pairs={{0,4},{4,0},{8,12},{12,8},{1,5},{5,1},{9,13},{13,9},{2,6},{6,2},{1... | collective-permute-start | bytes 1376264 | tf_op jit(solution)/shard_map/ppermute | solution.py:50
  8.0 16.0 %collective-permute-start.1 = (f32[28,32,128]{2,1,0:T(8,128)S(1)}, f32[28,32,128]{2,1,0:T(8,128)S(1)}, u32[]{:S(2)}, u32[]{:S(2)}) collective-permute-start(f32[28,32,128]{2,1,0:T(8,128)S(1)} %get-tuple-element.41), channel_id=1, source_target_pairs={{4,8},{8,4},{5,9},{9,5},{6,10},{10,6},{7,11},{11,7},{20,24},{24,20... | collective-permute-start | bytes 1376264 | tf_op jit(solution)/shard_map/ppermute | solution.py:50
  11.3 12.7 %collective-permute-start.4 = (f32[2,2,30,128]{3,2,1,0:T(8,128)S(1)}, f32[2,2,30,128]{3,2,1,0:T(8,128)S(1)}, u32[]{:S(2)}, u32[]{:S(2)}) collective-permute-start(f32[2,2,30,128]{3,2,1,0:T(8,128)S(1)} %get-tuple-element.45), channel_id=1, source_target_pairs={{0,4},{4,0},{8,12},{12,8},{1,5},{5,1},{9,13},{13,9},{2,6},{6,2},{1... | collective-permute-start | bytes 184328 | tf_op jit(solution)/shard_map/ppermute | solution.py:50
  15.2 8.8 %collective-permute-start.5 = (f32[2,2,30,128]{3,2,1,0:T(8,128)S(1)}, f32[2,2,30,128]{3,2,1,0:T(8,128)S(1)}, u32[]{:S(2)}, u32[]{:S(2)}) collective-permute-start(f32[2,2,30,128]{3,2,1,0:T(8,128)S(1)} %get-tuple-element.46), channel_id=1, source_target_pairs={{4,8},{8,4},{5,9},{9,5},{6,10},{10,6},{7,11},{11,7},{20,24},{24,20... | collective-permute-start | bytes 184328 | tf_op jit(solution)/shard_map/ppermute | solution.py:50

commit v3 on v2

--- a/solution.py
+++ b/solution.py
@@ -258,7 +258,7 @@
         self.turn(sweep, place(0), tiles)
         self.duals(sweep, place(0), tiles, extra)
         self.turn(sweep, place(1), tiles)
-        lax.fori_loop(1, count, step, 0)
+        lax.fori_loop(1, count, step, 0, unroll=2)
         project(count - 1)
 
 
@@ -341,7 +341,7 @@
 
 
 def rim_kernel(nx, ny, *refs):
-    x0, x1, c0, c1 = refs[:4]
+    x1, x0, c0, c1 = refs[:4]
     state = refs[4 + STATE + 1:4 + STATE + 1 + STATE]
     out, *scratch, rowed, sem = refs[4 + STATE + 1 + STATE:]
     costs, bounds = state[:2]
@@ -445,8 +445,8 @@
         in_specs=[VM] * 2, out_specs=[VM] * 2, out_shape=[edge_shape] * 2,
         compiler_params=params(), cost_estimate=work(1), name="edge",
     )(costs, bounds)
+    x1 = swap(m1, "gx", 1)
     x0 = swap(m0, "gx", 0)
-    x1 = swap(m1, "gx", 1)
 
     padded, plain = vmem(wide, LABELS, full + 2 * ROWS, lanes), vmem(wide, LABELS, full, lanes)
     shapes = [costs_shape, bounds_shape, padded, padded, padded, plain, plain, plain, plain, padded, plain]
@@ -484,7 +484,7 @@
         input_output_aliases={4 + i: i for i in range(STATE + 1)},
         scratch_shapes=scratch + [pltpu.VMEM((2 * HALO, LABELS, ny, lanes), jnp.float32), DMA((2 * HALO,))],
         compiler_params=params(), cost_estimate=work(10**11), name="rim",
-    )(x0, x1, d0, d1, *state)
+    )(x1, x0, d0, d1, *state)
     return state[-1]
 
 

time: 29.6 us -> 28.4 us (0.959)
  the two profiles are of different devices: /device:TPU:1 before, /device:TPU:9 now
where the time goes in v3:
time: 28.4 us; the launch traced here: 28.2 us
  Pallas kernels  17.2 us (61%)
  starting transfers between devices  10.9 us (38%)
    ppermute x6, starting transfers between devices, swap(): return lax.ppermute(value, axis, matching(lax.axis_size(axis), first))  10.9 us
    pallas_call x1, Pallas kernels, body(): pl.pallas_call(functools.partial(inner_kernel, nx, ny), in_specs=[VM] * (...  7.74 us
    pallas_call x1, Pallas kernels, body(): pl.pallas_call(functools.partial(rim_kernel, nx, ny), in_specs=[VM] * (4...  5.2 us
    pallas_call x1, Pallas kernels, body(): pl.pallas_call(functools.partial(start_kernel, nx, ny), in_specs=[VM] * 2...  2.25 us
    pallas_call x1, Pallas kernels, body(): pl.pallas_call(functools.partial(load_kernel, nx, ny), in_specs=[HB, HB],...  1.94 us
  transfers between devices with their start and end apart: 6, of which 0 were waited for; matrix products, arithmetic and copies ran while one was open for 0% of the time, Pallas kernels for 36%

profile of v3, /device:TPU:9, one launch (start us, length us, event | category | flops | bytes accessed | tf_op | source)
XLA Modules:
  0.0 28.2 jit_solution(9782648473068699961)
XLA Ops:
  0.0 1.9 %load.1 = (f32[22,7,40,128]{3,2,1,0:T(8,128)S(1)}, f32[22,3,40,128]{3,2,1,0:T(8,128)S(1)}, f32[16,30,128]{2,1,0:T(8,128)S(1)}, f32[16,30,128]{2,1,0:T(8,128)S(1)}) custom-call(s32[8,16,32,128]{3,2,1,0:T(8,128)} %u_hbm.1, s32[3,16,32,128]{3,2,1,0:T(8,128)} %a_hbm.1), custom_call_target="tpu_custom_call" | custom-call | flops 1 | tf_op jit(solution)/shard_map/load/pallas_call | solution.py:434
  1.9 0.7 %collective-permute-start.2 = (f32[16,30,128]{2,1,0:T(8,128)S(1)}, f32[16,30,128]{2,1,0:T(8,128)S(1)}, u32[]{:S(2)}, u32[]{:S(2)}) collective-permute-start(f32[16,30,128]{2,1,0:T(8,128)S(1)} %get-tuple-element.42), channel_id=1, source_target_pairs={{0,1},{1,0},{2,3},{3,2},{4,5},{5,4},{6,7},{7,6},{8,9},{9,8},{10,11... | collective-permute-start | bytes 737288 | tf_op jit(solution)/shard_map/ppermute | solution.py:50
  2.7 3.0 %collective-permute-start.3 = (f32[16,30,128]{2,1,0:T(8,128)S(1)}, f32[16,30,128]{2,1,0:T(8,128)S(1)}, u32[]{:S(2)}, u32[]{:S(2)}) collective-permute-start(f32[16,30,128]{2,1,0:T(8,128)S(1)} %get-tuple-element.43), channel_id=1, source_target_pairs={{1,2},{2,1},{5,6},{6,5},{9,10},{10,9},{13,14},{14,13},{17,18},{18,... | collective-permute-start | bytes 737288 | tf_op jit(solution)/shard_map/ppermute | solution.py:50
  5.7 0.1 edge.1
  5.8 3.2 %collective-permute-start = (f32[28,32,128]{2,1,0:T(8,128)S(1)}, f32[28,32,128]{2,1,0:T(8,128)S(1)}, u32[]{:S(2)}, u32[]{:S(2)}) collective-permute-start(f32[28,32,128]{2,1,0:T(8,128)S(1)} %get-tuple-element.40), channel_id=1, source_target_pairs={{4,8},{8,4},{5,9},{9,5},{6,10},{10,6},{7,11},{11,7},{20,24},{24,20... | collective-permute-start | bytes 1376264 | tf_op jit(solution)/shard_map/ppermute | solution.py:50
  9.0 0.1 collective-permute-start.1
  9.1 2.3 %start.1 = (f32[22,7,40,128]{3,2,1,0:T(8,128)S(1)}, f32[22,3,40,128]{3,2,1,0:T(8,128)S(1)}, f32[22,8,56,128]{3,2,1,0:T(8,128)S(1)}, f32[22,8,56,128]{3,2,1,0:T(8...) custom-call(f32[22,7,40,128]{3,2,1,0:T(8,128)S(1)} %get-tuple-elemen, ...), custom_call_target="tpu_custom_call", output_to_operand_aliasing={{0}: (0, {}), {1}: (1, {})} | custom-call | flops 1 | tf_op jit(solution)/shard_map/start/pallas_call | solution.py:456
  11.4 0.0 collective-permute-done.2.r0.refs_0_
  11.4 0.0 collective-permute-done.3.r1.refs_1_
  11.4 1.5 %collective-permute-start.4 = (f32[2,2,30,128]{3,2,1,0:T(8,128)S(1)}, f32[2,2,30,128]{3,2,1,0:T(8,128)S(1)}, u32[]{:S(2)}, u32[]{:S(2)}) collective-permute-start(f32[2,2,30,128]{3,2,1,0:T(8,128)S(1)} %get-tuple-element.45), channel_id=1, source_target_pairs={{0,4},{4,0},{8,12},{12,8},{1,5},{5,1},{9,13},{13,9},{2,6},{6,2},{1... | collective-permute-start | bytes 184328 | tf_op jit(solution)/shard_map/ppermute | solution.py:50
  12.9 2.3 %collective-permute-start.5 = (f32[2,2,30,128]{3,2,1,0:T(8,128)S(1)}, f32[2,2,30,128]{3,2,1,0:T(8,128)S(1)}, u32[]{:S(2)}, u32[]{:S(2)}) collective-permute-start(f32[2,2,30,128]{3,2,1,0:T(8,128)S(1)} %get-tuple-element.46), channel_id=1, source_target_pairs={{4,8},{8,4},{5,9},{9,5},{6,10},{10,6},{7,11},{11,7},{20,24},{24,20... | collective-permute-start | bytes 184328 | tf_op jit(solution)/shard_map/ppermute | solution.py:50
  15.2 7.7 %inner.1 = (f32[22,7,40,128]{3,2,1,0:T(8,128)S(1)}, f32[22,3,40,128]{3,2,1,0:T(8,128)S(1)}, f32[22,8,56,128]{3,2,1,0:T(8,128)S(1)}, f32[22,8,56,128]{3,2,1,0:T(8...) custom-call(f32[16,30,128]{2,1,0:T(8,128)S(1)} %collective-permute-d, ...), custom_call_target="tpu_custom_call", output_to_operand_aliasing={{0}: (2, {}), {1}: (3, {}), {2}: (4, {}), {3}: (5, {}), {4}... | custom-call | flops 99999997952 | tf_op jit(solution)/shard_map/inner/pallas_call | solution.py:473
  23.0 0.0 collective-permute-done.4.refs_2_
  23.0 0.0 collective-permute-done.5.refs_3_
  23.0 0.0 collective-permute-done.refs_0_
  23.0 0.0 collective-permute-done.1.refs_1_
  23.0 5.2 %rim.1 = (f32[22,7,40,128]{3,2,1,0:T(8,128)S(1)}, f32[22,3,40,128]{3,2,1,0:T(8,128)S(1)}, f32[22,8,56,128]{3,2,1,0:T(8,128)S(1)}, f32[22,8,56,128]{3,2,1,0:T(8,1...) custom-call(f32[28,32,128]{2,1,0:T(8,128)S(1)} %collective-permute-d, ...), custom_call_target="tpu_custom_call", output_to_operand_aliasing={{0}: (4, {}), {1}: (5, {}), {2}: (6, {}), {3}: (7, {}), {4}... | custom-call | flops 99999997952 | tf_op jit(solution)/shard_map/rim/pallas_call | solution.py:481
  (1 shorter events, 0.0 us)
Async XLA Ops:
  1.9 9.4 %collective-permute-start.2 = (f32[16,30,128]{2,1,0:T(8,128)S(1)}, f32[16,30,128]{2,1,0:T(8,128)S(1)}, u32[]{:S(2)}, u32[]{:S(2)}) collective-permute-start(f32[16,30,128]{2,1,0:T(8,128)S(1)} %get-tuple-element.42), channel_id=1, source_target_pairs={{0,1},{1,0},{2,3},{3,2},{4,5},{5,4},{6,7},{7,6},{8,9},{9,8},{10,11... | collective-permute-start | bytes 737288 | tf_op jit(solution)/shard_map/ppermute | solution.py:50
  2.7 8.7 %collective-permute-start.3 = (f32[16,30,128]{2,1,0:T(8,128)S(1)}, f32[16,30,128]{2,1,0:T(8,128)S(1)}, u32[]{:S(2)}, u32[]{:S(2)}) collective-permute-start(f32[16,30,128]{2,1,0:T(8,128)S(1)} %get-tuple-element.43), channel_id=1, source_target_pairs={{1,2},{2,1},{5,6},{6,5},{9,10},{10,9},{13,14},{14,13},{17,18},{18,... | collective-permute-start | bytes 737288 | tf_op jit(solution)/shard_map/ppermute | solution.py:50
  5.8 17.2 %collective-permute-start = (f32[28,32,128]{2,1,0:T(8,128)S(1)}, f32[28,32,128]{2,1,0:T(8,128)S(1)}, u32[]{:S(2)}, u32[]{:S(2)}) collective-permute-start(f32[28,32,128]{2,1,0:T(8,128)S(1)} %get-tuple-element.40), channel_id=1, source_target_pairs={{4,8},{8,4},{5,9},{9,5},{6,10},{10,6},{7,11},{11,7},{20,24},{24,20... | collective-permute-start | bytes 1376264 | tf_op jit(solution)/shard_map/ppermute | solution.py:50
  9.0 14.0 %collective-permute-start.1 = (f32[28,32,128]{2,1,0:T(8,128)S(1)}, f32[28,32,128]{2,1,0:T(8,128)S(1)}, u32[]{:S(2)}, u32[]{:S(2)}) collective-permute-start(f32[28,32,128]{2,1,0:T(8,128)S(1)} %get-tuple-element.41), channel_id=1, source_target_pairs={{0,4},{4,0},{8,12},{12,8},{1,5},{5,1},{9,13},{13,9},{2,6},{6,2},{1... | collective-permute-start | bytes 1376264 | tf_op jit(solution)/shard_map/ppermute | solution.py:50
  11.4 11.6 %collective-permute-start.4 = (f32[2,2,30,128]{3,2,1,0:T(8,128)S(1)}, f32[2,2,30,128]{3,2,1,0:T(8,128)S(1)}, u32[]{:S(2)}, u32[]{:S(2)}) collective-permute-start(f32[2,2,30,128]{3,2,1,0:T(8,128)S(1)} %get-tuple-element.45), channel_id=1, source_target_pairs={{0,4},{4,0},{8,12},{12,8},{1,5},{5,1},{9,13},{13,9},{2,6},{6,2},{1... | collective-permute-start | bytes 184328 | tf_op jit(solution)/shard_map/ppermute | solution.py:50
  12.9 10.1 %collective-permute-start.5 = (f32[2,2,30,128]{3,2,1,0:T(8,128)S(1)}, f32[2,2,30,128]{3,2,1,0:T(8,128)S(1)}, u32[]{:S(2)}, u32[]{:S(2)}) collective-permute-start(f32[2,2,30,128]{3,2,1,0:T(8,128)S(1)} %get-tuple-element.46), channel_id=1, source_target_pairs={{4,8},{8,4},{5,9},{9,5},{6,10},{10,6},{7,11},{11,7},{20,24},{24,20... | collective-permute-start | bytes 184328 | tf_op jit(solution)/shard_map/ppermute | solution.py:50

commit v4 on v3

--- a/solution.py
+++ b/solution.py
@@ -244,22 +244,39 @@
                     write(k, self.at(t), updated[k])
 
     def sweep(self, sweep, count, place, tiles, extra=(), write=None, written=None):
-        def project(i):
-            self.project(sweep, place(i), tiles, None if write is None else functools.partial(write, i))
-            if written is not None:
-                written(i)
-
         def step(i, _):
-            project(i - 1)
-            self.duals(sweep, place(i), tiles, extra)
-            self.turn(sweep, place(i + 1), tiles)
+            self.step(sweep, place, i, tiles, tiles, extra, write, written)
             return 0
 
         self.turn(sweep, place(0), tiles)
         self.duals(sweep, place(0), tiles, extra)
         self.turn(sweep, place(1), tiles)
         lax.fori_loop(1, count, step, 0, unroll=2)
-        project(count - 1)
+        self.step(sweep, place, count, tiles, (), (), write, written)
+
+    def step(self, sweep, place, i, done, tiles, extra, write, written):
+        self.project(sweep, place(i - 1), done, None if write is None else functools.partial(write, i - 1))
+        if written is not None:
+            written(i - 1)
+        if tiles:
+            self.duals(sweep, place(i), tiles, extra)
+            self.turn(sweep, place(i + 1), tiles)
+
+    def rim_sweep(self, sweep, count, place, write=None, written=None):
+        own, last = range(self.tiles - 1), self.tiles - 1
+        most = range(self.tiles) if sweep < 2 else own
+        extra = () if sweep < 2 else (last,)
+        for t in own:
+            self.step_x(sweep, place(0) - 1, t)
+        if sweep < 2:
+            self.step_x(sweep, place(0), last)
+        self.turn(sweep, place(0), own)
+        self.duals(sweep, place(0), own, (last,))
+        self.turn(sweep, place(1), most)
+        for i in range(1, count + 1):
+            done = own if i in (1, count) else most
+            tiles = () if i == count else own if i == count - 1 else most
+            self.step(sweep, place, i, done, tiles, (last,) if tiles == own else extra, write, written)
 
 
 def scratch_fields(rows, lanes):
@@ -346,6 +363,7 @@
     out, *scratch, rowed, sem = refs[4 + STATE + 1 + STATE:]
     costs, bounds = state[:2]
     tiles = ny // ROWS + 1
+    wide = nx + 2 * HALO
     everything = range(tiles)
     field = Field(tiles, scratch, *state)
     odd_x = lax.rem(lax.axis_index("gx"), 2)
@@ -388,13 +406,16 @@
         fill(x0, c0, 0, 1)
 
     def place(i, left, right):
-        return jnp.where(i < HALO, left + i, right + i - HALO)
+        return left + i if i < HALO else right + i - HALO
+
+    field.begin(0, range(tiles - 1))
+    field.begin(wide - 1, range(tiles - 1))
 
     def begin(i, _):
-        field.begin(place(i, 0, HALO + nx), everything)
+        field.begin(jnp.where(i < HALO, i, wide - 2 * HALO + i), everything)
         return 0
 
-    lax.fori_loop(0, 2 * HALO, begin, 0)
+    lax.fori_loop(1, 2 * HALO - 1, begin, 0)
 
     def write(i, k, rows, value):
         rowed[i, k, rows] = value
@@ -404,19 +425,13 @@
 
     for sweep in range(3):
         at = functools.partial(place, left=1 + sweep, right=nx + HALO - 1 - sweep)
-        used = everything if sweep < 2 else range(tiles - 1)
-        for t in used:
-            field.step_x(sweep, sweep, t)
         if sweep < 2:
-            field.sweep(sweep, 2 * HALO, at, used)
+            field.rim_sweep(sweep, 2 * HALO, at)
         else:
-            field.sweep(sweep, 2 * HALO, at, used, (tiles - 1,), write, lambda i: flush(i).start())
-
-    def finish(i, _):
+            field.rim_sweep(sweep, 2 * HALO, at, write, lambda i: flush(i).start())
+
+    for i in range(2 * HALO):
         flush(i).wait()
-        return 0
-
-    lax.fori_loop(0, 2 * HALO, finish, 0)
 
 
 def vmem(*shape):

time: 28.4 us -> 27.8 us (0.979)
  Pallas kernels: 17.2 us -> 16.7 us
    pallas_call x1, Pallas kernels: 5.2 us -> 4.63 us  [body(): pl.pallas_call(functools.partial(rim_kernel, nx, ny), in_specs=[VM] * (4...]
where the time goes in v4:
time: 27.8 us; the launch traced here: 27.7 us
  Pallas kernels  16.7 us (60%)
  starting transfers between devices  10.9 us (39%)
    ppermute x6, starting transfers between devices, swap(): return lax.ppermute(value, axis, matching(lax.axis_size(axis), first))  10.9 us
    pallas_call x1, Pallas kernels, body(): pl.pallas_call(functools.partial(inner_kernel, nx, ny), in_specs=[VM] * (...  7.74 us
    pallas_call x1, Pallas kernels, body(): pl.pallas_call(functools.partial(rim_kernel, nx, ny), in_specs=[VM] * (4...  4.63 us
    pallas_call x1, Pallas kernels, body(): pl.pallas_call(functools.partial(start_kernel, nx, ny), in_specs=[VM] * 2...  2.25 us
    pallas_call x1, Pallas kernels, body(): pl.pallas_call(functools.partial(load_kernel, nx, ny), in_specs=[HB, HB],...  1.94 us
  transfers between devices with their start and end apart: 6, of which 0 were waited for; matrix products, arithmetic and copies ran while one was open for 0% of the time, Pallas kernels for 36%

profile of v4, /device:TPU:9, one launch (start us, length us, event | category | flops | bytes accessed | tf_op | source)
XLA Modules:
  0.0 27.7 jit_solution(4834126122116354227)
XLA Ops:
  0.0 1.9 %load.1 = (f32[22,7,40,128]{3,2,1,0:T(8,128)S(1)}, f32[22,3,40,128]{3,2,1,0:T(8,128)S(1)}, f32[16,30,128]{2,1,0:T(8,128)S(1)}, f32[16,30,128]{2,1,0:T(8,128)S(1)}) custom-call(s32[8,16,32,128]{3,2,1,0:T(8,128)} %u_hbm.1, s32[3,16,32,128]{3,2,1,0:T(8,128)} %a_hbm.1), custom_call_target="tpu_custom_call" | custom-call | flops 1 | tf_op jit(solution)/shard_map/load/pallas_call | solution.py:449
  1.9 0.7 %collective-permute-start.2 = (f32[16,30,128]{2,1,0:T(8,128)S(1)}, f32[16,30,128]{2,1,0:T(8,128)S(1)}, u32[]{:S(2)}, u32[]{:S(2)}) collective-permute-start(f32[16,30,128]{2,1,0:T(8,128)S(1)} %get-tuple-element.42), channel_id=1, source_target_pairs={{0,1},{1,0},{2,3},{3,2},{4,5},{5,4},{6,7},{7,6},{8,9},{9,8},{10,11... | collective-permute-start | bytes 737288 | tf_op jit(solution)/shard_map/ppermute | solution.py:50
  2.7 3.0 %collective-permute-start.3 = (f32[16,30,128]{2,1,0:T(8,128)S(1)}, f32[16,30,128]{2,1,0:T(8,128)S(1)}, u32[]{:S(2)}, u32[]{:S(2)}) collective-permute-start(f32[16,30,128]{2,1,0:T(8,128)S(1)} %get-tuple-element.43), channel_id=1, source_target_pairs={{1,2},{2,1},{5,6},{6,5},{9,10},{10,9},{13,14},{14,13},{17,18},{18,... | collective-permute-start | bytes 737288 | tf_op jit(solution)/shard_map/ppermute | solution.py:50
  5.7 0.1 edge.1
  5.8 3.2 %collective-permute-start = (f32[28,32,128]{2,1,0:T(8,128)S(1)}, f32[28,32,128]{2,1,0:T(8,128)S(1)}, u32[]{:S(2)}, u32[]{:S(2)}) collective-permute-start(f32[28,32,128]{2,1,0:T(8,128)S(1)} %get-tuple-element.40), channel_id=1, source_target_pairs={{4,8},{8,4},{5,9},{9,5},{6,10},{10,6},{7,11},{11,7},{20,24},{24,20... | collective-permute-start | bytes 1376264 | tf_op jit(solution)/shard_map/ppermute | solution.py:50
  9.0 0.1 collective-permute-start.1
  9.1 2.3 %start.1 = (f32[22,7,40,128]{3,2,1,0:T(8,128)S(1)}, f32[22,3,40,128]{3,2,1,0:T(8,128)S(1)}, f32[22,8,56,128]{3,2,1,0:T(8,128)S(1)}, f32[22,8,56,128]{3,2,1,0:T(8...) custom-call(f32[22,7,40,128]{3,2,1,0:T(8,128)S(1)} %get-tuple-elemen, ...), custom_call_target="tpu_custom_call", output_to_operand_aliasing={{0}: (0, {}), {1}: (1, {})} | custom-call | flops 1 | tf_op jit(solution)/shard_map/start/pallas_call | solution.py:471
  11.4 0.0 collective-permute-done.2.r0.refs_0_
  11.4 0.0 collective-permute-done.3.r1.refs_1_
  11.4 1.5 %collective-permute-start.4 = (f32[2,2,30,128]{3,2,1,0:T(8,128)S(1)}, f32[2,2,30,128]{3,2,1,0:T(8,128)S(1)}, u32[]{:S(2)}, u32[]{:S(2)}) collective-permute-start(f32[2,2,30,128]{3,2,1,0:T(8,128)S(1)} %get-tuple-element.45), channel_id=1, source_target_pairs={{0,4},{4,0},{8,12},{12,8},{1,5},{5,1},{9,13},{13,9},{2,6},{6,2},{1... | collective-permute-start | bytes 184328 | tf_op jit(solution)/shard_map/ppermute | solution.py:50
  12.9 2.3 %collective-permute-start.5 = (f32[2,2,30,128]{3,2,1,0:T(8,128)S(1)}, f32[2,2,30,128]{3,2,1,0:T(8,128)S(1)}, u32[]{:S(2)}, u32[]{:S(2)}) collective-permute-start(f32[2,2,30,128]{3,2,1,0:T(8,128)S(1)} %get-tuple-element.46), channel_id=1, source_target_pairs={{4,8},{8,4},{5,9},{9,5},{6,10},{10,6},{7,11},{11,7},{20,24},{24,20... | collective-permute-start | bytes 184328 | tf_op jit(solution)/shard_map/ppermute | solution.py:50
  15.2 7.7 %inner.1 = (f32[22,7,40,128]{3,2,1,0:T(8,128)S(1)}, f32[22,3,40,128]{3,2,1,0:T(8,128)S(1)}, f32[22,8,56,128]{3,2,1,0:T(8,128)S(1)}, f32[22,8,56,128]{3,2,1,0:T(8...) custom-call(f32[16,30,128]{2,1,0:T(8,128)S(1)} %collective-permute-d, ...), custom_call_target="tpu_custom_call", output_to_operand_aliasing={{0}: (2, {}), {1}: (3, {}), {2}: (4, {}), {3}: (5, {}), {4}... | custom-call | flops 99999997952 | tf_op jit(solution)/shard_map/inner/pallas_call | solution.py:488
  23.0 0.0 collective-permute-done.4.refs_2_
  23.0 0.0 collective-permute-done.5.refs_3_
  23.0 0.0 collective-permute-done.refs_0_
  23.0 0.0 collective-permute-done.1.refs_1_
  23.0 4.6 %rim.1 = (f32[22,7,40,128]{3,2,1,0:T(8,128)S(1)}, f32[22,3,40,128]{3,2,1,0:T(8,128)S(1)}, f32[22,8,56,128]{3,2,1,0:T(8,128)S(1)}, f32[22,8,56,128]{3,2,1,0:T(8,1...) custom-call(f32[28,32,128]{2,1,0:T(8,128)S(1)} %collective-permute-d, ...), custom_call_target="tpu_custom_call", output_to_operand_aliasing={{0}: (4, {}), {1}: (5, {}), {2}: (6, {}), {3}: (7, {}), {4}... | custom-call | flops 99999997952 | tf_op jit(solution)/shard_map/rim/pallas_call | solution.py:496
  (1 shorter events, 0.0 us)
Async XLA Ops:
  1.9 9.4 %collective-permute-start.2 = (f32[16,30,128]{2,1,0:T(8,128)S(1)}, f32[16,30,128]{2,1,0:T(8,128)S(1)}, u32[]{:S(2)}, u32[]{:S(2)}) collective-permute-start(f32[16,30,128]{2,1,0:T(8,128)S(1)} %get-tuple-element.42), channel_id=1, source_target_pairs={{0,1},{1,0},{2,3},{3,2},{4,5},{5,4},{6,7},{7,6},{8,9},{9,8},{10,11... | collective-permute-start | bytes 737288 | tf_op jit(solution)/shard_map/ppermute | solution.py:50
  2.7 8.7 %collective-permute-start.3 = (f32[16,30,128]{2,1,0:T(8,128)S(1)}, f32[16,30,128]{2,1,0:T(8,128)S(1)}, u32[]{:S(2)}, u32[]{:S(2)}) collective-permute-start(f32[16,30,128]{2,1,0:T(8,128)S(1)} %get-tuple-element.43), channel_id=1, source_target_pairs={{1,2},{2,1},{5,6},{6,5},{9,10},{10,9},{13,14},{14,13},{17,18},{18,... | collective-permute-start | bytes 737288 | tf_op jit(solution)/shard_map/ppermute | solution.py:50
  5.8 17.2 %collective-permute-start = (f32[28,32,128]{2,1,0:T(8,128)S(1)}, f32[28,32,128]{2,1,0:T(8,128)S(1)}, u32[]{:S(2)}, u32[]{:S(2)}) collective-permute-start(f32[28,32,128]{2,1,0:T(8,128)S(1)} %get-tuple-element.40), channel_id=1, source_target_pairs={{4,8},{8,4},{5,9},{9,5},{6,10},{10,6},{7,11},{11,7},{20,24},{24,20... | collective-permute-start | bytes 1376264 | tf_op jit(solution)/shard_map/ppermute | solution.py:50
  9.0 14.0 %collective-permute-start.1 = (f32[28,32,128]{2,1,0:T(8,128)S(1)}, f32[28,32,128]{2,1,0:T(8,128)S(1)}, u32[]{:S(2)}, u32[]{:S(2)}) collective-permute-start(f32[28,32,128]{2,1,0:T(8,128)S(1)} %get-tuple-element.41), channel_id=1, source_target_pairs={{0,4},{4,0},{8,12},{12,8},{1,5},{5,1},{9,13},{13,9},{2,6},{6,2},{1... | collective-permute-start | bytes 1376264 | tf_op jit(solution)/shard_map/ppermute | solution.py:50
  11.4 11.6 %collective-permute-start.4 = (f32[2,2,30,128]{3,2,1,0:T(8,128)S(1)}, f32[2,2,30,128]{3,2,1,0:T(8,128)S(1)}, u32[]{:S(2)}, u32[]{:S(2)}) collective-permute-start(f32[2,2,30,128]{3,2,1,0:T(8,128)S(1)} %get-tuple-element.45), channel_id=1, source_target_pairs={{0,4},{4,0},{8,12},{12,8},{1,5},{5,1},{9,13},{13,9},{2,6},{6,2},{1... | collective-permute-start | bytes 184328 | tf_op jit(solution)/shard_map/ppermute | solution.py:50
  12.9 10.1 %collective-permute-start.5 = (f32[2,2,30,128]{3,2,1,0:T(8,128)S(1)}, f32[2,2,30,128]{3,2,1,0:T(8,128)S(1)}, u32[]{:S(2)}, u32[]{:S(2)}) collective-permute-start(f32[2,2,30,128]{3,2,1,0:T(8,128)S(1)} %get-tuple-element.46), channel_id=1, source_target_pairs={{4,8},{8,4},{5,9},{9,5},{6,10},{10,6},{7,11},{11,7},{20,24},{24,20... | collective-permute-start | bytes 184328 | tf_op jit(solution)/shard_map/ppermute | solution.py:50

commit v5 on v4

--- a/solution.py
+++ b/solution.py
@@ -243,7 +243,7 @@
                 else:
                     write(k, self.at(t), updated[k])
 
-    def sweep(self, sweep, count, place, tiles, extra=(), write=None, written=None):
+    def sweep(self, sweep, count, place, tiles, extra=(), write=None, written=None, unroll=True):
         def step(i, _):
             self.step(sweep, place, i, tiles, tiles, extra, write, written)
             return 0
@@ -251,7 +251,11 @@
         self.turn(sweep, place(0), tiles)
         self.duals(sweep, place(0), tiles, extra)
         self.turn(sweep, place(1), tiles)
-        lax.fori_loop(1, count, step, 0, unroll=2)
+        if unroll:
+            for i in range(1, count):
+                step(i, 0)
+        else:
+            lax.fori_loop(1, count, step, 0, unroll=2)
         self.step(sweep, place, count, tiles, (), (), write, written)
 
     def step(self, sweep, place, i, done, tiles, extra, write, written):
@@ -300,7 +304,7 @@
     inner = range(1, tiles - 2)
     for t in inner:
         field.step_x(0, HALO, t)
-    field.sweep(0, nx - 2, lambda i: HALO + 1 + i, inner, extra=(0,))
+    field.sweep(0, nx - 2, lambda i: HALO + 1 + i, inner, extra=(0,), unroll=False)
 
 
 def inner_kernel(nx, ny, *refs):

time: 27.8 us -> 27.6 us (level)
  Pallas kernels: 16.7 us -> 16.4 us
where the time goes in v5:
time: 27.6 us; the launch traced here: 27.4 us
  Pallas kernels  16.4 us (59%)
  starting transfers between devices  10.9 us (39%)
    ppermute x6, starting transfers between devices, swap(): return lax.ppermute(value, axis, matching(lax.axis_size(axis), first))  10.9 us
    pallas_call x1, Pallas kernels, body(): pl.pallas_call(functools.partial(inner_kernel, nx, ny), in_specs=[VM] * (...  7.51 us
    pallas_call x1, Pallas kernels, body(): pl.pallas_call(functools.partial(rim_kernel, nx, ny), in_specs=[VM] * (4...  4.63 us
    pallas_call x1, Pallas kernels, body(): pl.pallas_call(functools.partial(start_kernel, nx, ny), in_specs=[VM] * 2...  2.25 us
    pallas_call x1, Pallas kernels, body(): pl.pallas_call(functools.partial(load_kernel, nx, ny), in_specs=[HB, HB],...  1.94 us
  transfers between devices with their start and end apart: 6, of which 0 were waited for; matrix products, arithmetic and copies ran while one was open for 0% of the time, Pallas kernels for 36%

profile of v5, /device:TPU:9, one launch (start us, length us, event | category | flops | bytes accessed | tf_op | source)
XLA Modules:
  0.0 27.4 jit_solution(7982856957489537547)
XLA Ops:
  0.0 1.9 %load.1 = (f32[22,7,40,128]{3,2,1,0:T(8,128)S(1)}, f32[22,3,40,128]{3,2,1,0:T(8,128)S(1)}, f32[16,30,128]{2,1,0:T(8,128)S(1)}, f32[16,30,128]{2,1,0:T(8,128)S(1)}) custom-call(s32[8,16,32,128]{3,2,1,0:T(8,128)} %u_hbm.1, s32[3,16,32,128]{3,2,1,0:T(8,128)} %a_hbm.1), custom_call_target="tpu_custom_call" | custom-call | flops 1 | tf_op jit(solution)/shard_map/load/pallas_call | solution.py:453
  1.9 0.7 %collective-permute-start.2 = (f32[16,30,128]{2,1,0:T(8,128)S(1)}, f32[16,30,128]{2,1,0:T(8,128)S(1)}, u32[]{:S(2)}, u32[]{:S(2)}) collective-permute-start(f32[16,30,128]{2,1,0:T(8,128)S(1)} %get-tuple-element.42), channel_id=1, source_target_pairs={{0,1},{1,0},{2,3},{3,2},{4,5},{5,4},{6,7},{7,6},{8,9},{9,8},{10,11... | collective-permute-start | bytes 737288 | tf_op jit(solution)/shard_map/ppermute | solution.py:50
  2.7 3.0 %collective-permute-start.3 = (f32[16,30,128]{2,1,0:T(8,128)S(1)}, f32[16,30,128]{2,1,0:T(8,128)S(1)}, u32[]{:S(2)}, u32[]{:S(2)}) collective-permute-start(f32[16,30,128]{2,1,0:T(8,128)S(1)} %get-tuple-element.43), channel_id=1, source_target_pairs={{1,2},{2,1},{5,6},{6,5},{9,10},{10,9},{13,14},{14,13},{17,18},{18,... | collective-permute-start | bytes 737288 | tf_op jit(solution)/shard_map/ppermute | solution.py:50
  5.7 0.1 edge.1
  5.8 3.2 %collective-permute-start = (f32[28,32,128]{2,1,0:T(8,128)S(1)}, f32[28,32,128]{2,1,0:T(8,128)S(1)}, u32[]{:S(2)}, u32[]{:S(2)}) collective-permute-start(f32[28,32,128]{2,1,0:T(8,128)S(1)} %get-tuple-element.40), channel_id=1, source_target_pairs={{4,8},{8,4},{5,9},{9,5},{6,10},{10,6},{7,11},{11,7},{20,24},{24,20... | collective-permute-start | bytes 1376264 | tf_op jit(solution)/shard_map/ppermute | solution.py:50
  9.0 0.1 collective-permute-start.1
  9.1 2.3 %start.1 = (f32[22,7,40,128]{3,2,1,0:T(8,128)S(1)}, f32[22,3,40,128]{3,2,1,0:T(8,128)S(1)}, f32[22,8,56,128]{3,2,1,0:T(8,128)S(1)}, f32[22,8,56,128]{3,2,1,0:T(8...) custom-call(f32[22,7,40,128]{3,2,1,0:T(8,128)S(1)} %get-tuple-elemen, ...), custom_call_target="tpu_custom_call", output_to_operand_aliasing={{0}: (0, {}), {1}: (1, {})} | custom-call | flops 1 | tf_op jit(solution)/shard_map/start/pallas_call | solution.py:475
  11.4 0.0 collective-permute-done.2.r0.refs_0_
  11.4 0.0 collective-permute-done.3.r1.refs_1_
  11.4 1.5 %collective-permute-start.4 = (f32[2,2,30,128]{3,2,1,0:T(8,128)S(1)}, f32[2,2,30,128]{3,2,1,0:T(8,128)S(1)}, u32[]{:S(2)}, u32[]{:S(2)}) collective-permute-start(f32[2,2,30,128]{3,2,1,0:T(8,128)S(1)} %get-tuple-element.45), channel_id=1, source_target_pairs={{0,4},{4,0},{8,12},{12,8},{1,5},{5,1},{9,13},{13,9},{2,6},{6,2},{1... | collective-permute-start | bytes 184328 | tf_op jit(solution)/shard_map/ppermute | solution.py:50
  12.9 2.3 %collective-permute-start.5 = (f32[2,2,30,128]{3,2,1,0:T(8,128)S(1)}, f32[2,2,30,128]{3,2,1,0:T(8,128)S(1)}, u32[]{:S(2)}, u32[]{:S(2)}) collective-permute-start(f32[2,2,30,128]{3,2,1,0:T(8,128)S(1)} %get-tuple-element.46), channel_id=1, source_target_pairs={{4,8},{8,4},{5,9},{9,5},{6,10},{10,6},{7,11},{11,7},{20,24},{24,20... | collective-permute-start | bytes 184328 | tf_op jit(solution)/shard_map/ppermute | solution.py:50
  15.2 7.5 %inner.1 = (f32[22,7,40,128]{3,2,1,0:T(8,128)S(1)}, f32[22,3,40,128]{3,2,1,0:T(8,128)S(1)}, f32[22,8,56,128]{3,2,1,0:T(8,128)S(1)}, f32[22,8,56,128]{3,2,1,0:T(8...) custom-call(f32[16,30,128]{2,1,0:T(8,128)S(1)} %collective-permute-d, ...), custom_call_target="tpu_custom_call", output_to_operand_aliasing={{0}: (2, {}), {1}: (3, {}), {2}: (4, {}), {3}: (5, {}), {4}... | custom-call | flops 99999997952 | tf_op jit(solution)/shard_map/inner/pallas_call | solution.py:492
  22.8 0.0 collective-permute-done.4.refs_2_
  22.8 0.0 collective-permute-done.5.refs_3_
  22.8 0.0 collective-permute-done.refs_0_
  22.8 0.0 collective-permute-done.1.refs_1_
  22.8 4.6 %rim.1 = (f32[22,7,40,128]{3,2,1,0:T(8,128)S(1)}, f32[22,3,40,128]{3,2,1,0:T(8,128)S(1)}, f32[22,8,56,128]{3,2,1,0:T(8,128)S(1)}, f32[22,8,56,128]{3,2,1,0:T(8,1...) custom-call(f32[28,32,128]{2,1,0:T(8,128)S(1)} %collective-permute-d, ...), custom_call_target="tpu_custom_call", output_to_operand_aliasing={{0}: (4, {}), {1}: (5, {}), {2}: (6, {}), {3}: (7, {}), {4}... | custom-call | flops 99999997952 | tf_op jit(solution)/shard_map/rim/pallas_call | solution.py:500
  (1 shorter events, 0.0 us)
Async XLA Ops:
  1.9 9.4 %collective-permute-start.2 = (f32[16,30,128]{2,1,0:T(8,128)S(1)}, f32[16,30,128]{2,1,0:T(8,128)S(1)}, u32[]{:S(2)}, u32[]{:S(2)}) collective-permute-start(f32[16,30,128]{2,1,0:T(8,128)S(1)} %get-tuple-element.42), channel_id=1, source_target_pairs={{0,1},{1,0},{2,3},{3,2},{4,5},{5,4},{6,7},{7,6},{8,9},{9,8},{10,11... | collective-permute-start | bytes 737288 | tf_op jit(solution)/shard_map/ppermute | solution.py:50
  2.7 8.7 %collective-permute-start.3 = (f32[16,30,128]{2,1,0:T(8,128)S(1)}, f32[16,30,128]{2,1,0:T(8,128)S(1)}, u32[]{:S(2)}, u32[]{:S(2)}) collective-permute-start(f32[16,30,128]{2,1,0:T(8,128)S(1)} %get-tuple-element.43), channel_id=1, source_target_pairs={{1,2},{2,1},{5,6},{6,5},{9,10},{10,9},{13,14},{14,13},{17,18},{18,... | collective-permute-start | bytes 737288 | tf_op jit(solution)/shard_map/ppermute | solution.py:50
  5.8 17.0 %collective-permute-start = (f32[28,32,128]{2,1,0:T(8,128)S(1)}, f32[28,32,128]{2,1,0:T(8,128)S(1)}, u32[]{:S(2)}, u32[]{:S(2)}) collective-permute-start(f32[28,32,128]{2,1,0:T(8,128)S(1)} %get-tuple-element.40), channel_id=1, source_target_pairs={{4,8},{8,4},{5,9},{9,5},{6,10},{10,6},{7,11},{11,7},{20,24},{24,20... | collective-permute-start | bytes 1376264 | tf_op jit(solution)/shard_map/ppermute | solution.py:50
  9.0 13.8 %collective-permute-start.1 = (f32[28,32,128]{2,1,0:T(8,128)S(1)}, f32[28,32,128]{2,1,0:T(8,128)S(1)}, u32[]{:S(2)}, u32[]{:S(2)}) collective-permute-start(f32[28,32,128]{2,1,0:T(8,128)S(1)} %get-tuple-element.41), channel_id=1, source_target_pairs={{0,4},{4,0},{8,12},{12,8},{1,5},{5,1},{9,13},{13,9},{2,6},{6,2},{1... | collective-permute-start | bytes 1376264 | tf_op jit(solution)/shard_map/ppermute | solution.py:50
  11.4 11.3 %collective-permute-start.4 = (f32[2,2,30,128]{3,2,1,0:T(8,128)S(1)}, f32[2,2,30,128]{3,2,1,0:T(8,128)S(1)}, u32[]{:S(2)}, u32[]{:S(2)}) collective-permute-start(f32[2,2,30,128]{3,2,1,0:T(8,128)S(1)} %get-tuple-element.45), channel_id=1, source_target_pairs={{0,4},{4,0},{8,12},{12,8},{1,5},{5,1},{9,13},{13,9},{2,6},{6,2},{1... | collective-permute-start | bytes 184328 | tf_op jit(solution)/shard_map/ppermute | solution.py:50
  12.9 9.8 %collective-permute-start.5 = (f32[2,2,30,128]{3,2,1,0:T(8,128)S(1)}, f32[2,2,30,128]{3,2,1,0:T(8,128)S(1)}, u32[]{:S(2)}, u32[]{:S(2)}) collective-permute-start(f32[2,2,30,128]{3,2,1,0:T(8,128)S(1)} %get-tuple-element.46), channel_id=1, source_target_pairs={{4,8},{8,4},{5,9},{9,5},{6,10},{10,6},{7,11},{11,7},{20,24},{24,20... | collective-permute-start | bytes 184328 | tf_op jit(solution)/shard_map/ppermute | solution.py:50

commit v6 on v5

--- a/solution.py
+++ b/solution.py
@@ -321,7 +321,7 @@
         def step(x, _):
             put_rows(ny, costs, bounds, x + HALO, ahead.at[x], behind.at[x])
             return 0
-        lax.fori_loop(0, nx, step, 0)
+        lax.fori_loop(0, nx, step, 0, unroll=2)
 
     @pl.when(odd == 0)
     def _():
@@ -335,7 +335,7 @@
         field.begin(x, [tiles - 1])
         return 0
 
-    lax.fori_loop(HALO, HALO + nx, begin, 0)
+    lax.fori_loop(HALO, HALO + nx, begin, 0, unroll=4)
     outer = [0, tiles - 2, tiles - 1]
     for t in outer:
         field.step_x(0, HALO, t)

time: 27.6 us -> 27.4 us (level)
  transfers between devices with their start and end apart: 6 -> 6, of which waited for: 0 -> 0; matrix products, arithmetic and copies ran while one was open for 0% -> 0% of each run, Pallas kernels for 36% -> 35%
where the time goes in v6:
time: 27.4 us; the launch traced here: 27.2 us
  Pallas kernels  16.2 us (59%)
  starting transfers between devices  10.9 us (40%)
    ppermute x6, starting transfers between devices, swap(): return lax.ppermute(value, axis, matching(lax.axis_size(axis), first))  10.9 us
    pallas_call x1, Pallas kernels, body(): pl.pallas_call(functools.partial(inner_kernel, nx, ny), in_specs=[VM] * (...  7.29 us
    pallas_call x1, Pallas kernels, body(): pl.pallas_call(functools.partial(rim_kernel, nx, ny), in_specs=[VM] * (4...  4.63 us
    pallas_call x1, Pallas kernels, body(): pl.pallas_call(functools.partial(start_kernel, nx, ny), in_specs=[VM] * 2...  2.25 us
    pallas_call x1, Pallas kernels, body(): pl.pallas_call(functools.partial(load_kernel, nx, ny), in_specs=[HB, HB],...  1.94 us
  transfers between devices with their start and end apart: 6, of which 0 were waited for; matrix products, arithmetic and copies ran while one was open for 0% of the time, Pallas kernels for 35%

profile of v6, /device:TPU:9, one launch (start us, length us, event | category | flops | bytes accessed | tf_op | source)
XLA Modules:
  0.0 27.2 jit_solution(9652807038757474688)
XLA Ops:
  0.0 1.9 %load.1 = (f32[22,7,40,128]{3,2,1,0:T(8,128)S(1)}, f32[22,3,40,128]{3,2,1,0:T(8,128)S(1)}, f32[16,30,128]{2,1,0:T(8,128)S(1)}, f32[16,30,128]{2,1,0:T(8,128)S(1)}) custom-call(s32[8,16,32,128]{3,2,1,0:T(8,128)} %u_hbm.1, s32[3,16,32,128]{3,2,1,0:T(8,128)} %a_hbm.1), custom_call_target="tpu_custom_call" | custom-call | flops 1 | tf_op jit(solution)/shard_map/load/pallas_call | solution.py:453
  1.9 0.7 %collective-permute-start.2 = (f32[16,30,128]{2,1,0:T(8,128)S(1)}, f32[16,30,128]{2,1,0:T(8,128)S(1)}, u32[]{:S(2)}, u32[]{:S(2)}) collective-permute-start(f32[16,30,128]{2,1,0:T(8,128)S(1)} %get-tuple-element.42), channel_id=1, source_target_pairs={{0,1},{1,0},{2,3},{3,2},{4,5},{5,4},{6,7},{7,6},{8,9},{9,8},{10,11... | collective-permute-start | bytes 737288 | tf_op jit(solution)/shard_map/ppermute | solution.py:50
  2.7 3.0 %collective-permute-start.3 = (f32[16,30,128]{2,1,0:T(8,128)S(1)}, f32[16,30,128]{2,1,0:T(8,128)S(1)}, u32[]{:S(2)}, u32[]{:S(2)}) collective-permute-start(f32[16,30,128]{2,1,0:T(8,128)S(1)} %get-tuple-element.43), channel_id=1, source_target_pairs={{1,2},{2,1},{5,6},{6,5},{9,10},{10,9},{13,14},{14,13},{17,18},{18,... | collective-permute-start | bytes 737288 | tf_op jit(solution)/shard_map/ppermute | solution.py:50
  5.7 0.1 edge.1
  5.8 3.2 %collective-permute-start = (f32[28,32,128]{2,1,0:T(8,128)S(1)}, f32[28,32,128]{2,1,0:T(8,128)S(1)}, u32[]{:S(2)}, u32[]{:S(2)}) collective-permute-start(f32[28,32,128]{2,1,0:T(8,128)S(1)} %get-tuple-element.40), channel_id=1, source_target_pairs={{4,8},{8,4},{5,9},{9,5},{6,10},{10,6},{7,11},{11,7},{20,24},{24,20... | collective-permute-start | bytes 1376264 | tf_op jit(solution)/shard_map/ppermute | solution.py:50
  9.0 0.1 collective-permute-start.1
  9.1 2.3 %start.1 = (f32[22,7,40,128]{3,2,1,0:T(8,128)S(1)}, f32[22,3,40,128]{3,2,1,0:T(8,128)S(1)}, f32[22,8,56,128]{3,2,1,0:T(8,128)S(1)}, f32[22,8,56,128]{3,2,1,0:T(8...) custom-call(f32[22,7,40,128]{3,2,1,0:T(8,128)S(1)} %get-tuple-elemen, ...), custom_call_target="tpu_custom_call", output_to_operand_aliasing={{0}: (0, {}), {1}: (1, {})} | custom-call | flops 1 | tf_op jit(solution)/shard_map/start/pallas_call | solution.py:475
  11.4 0.0 collective-permute-done.2.r0.refs_0_
  11.4 0.0 collective-permute-done.3.r1.refs_1_
  11.4 1.5 %collective-permute-start.4 = (f32[2,2,30,128]{3,2,1,0:T(8,128)S(1)}, f32[2,2,30,128]{3,2,1,0:T(8,128)S(1)}, u32[]{:S(2)}, u32[]{:S(2)}) collective-permute-start(f32[2,2,30,128]{3,2,1,0:T(8,128)S(1)} %get-tuple-element.45), channel_id=1, source_target_pairs={{0,4},{4,0},{8,12},{12,8},{1,5},{5,1},{9,13},{13,9},{2,6},{6,2},{1... | collective-permute-start | bytes 184328 | tf_op jit(solution)/shard_map/ppermute | solution.py:50
  12.9 2.3 %collective-permute-start.5 = (f32[2,2,30,128]{3,2,1,0:T(8,128)S(1)}, f32[2,2,30,128]{3,2,1,0:T(8,128)S(1)}, u32[]{:S(2)}, u32[]{:S(2)}) collective-permute-start(f32[2,2,30,128]{3,2,1,0:T(8,128)S(1)} %get-tuple-element.46), channel_id=1, source_target_pairs={{4,8},{8,4},{5,9},{9,5},{6,10},{10,6},{7,11},{11,7},{20,24},{24,20... | collective-permute-start | bytes 184328 | tf_op jit(solution)/shard_map/ppermute | solution.py:50
  15.2 7.3 %inner.1 = (f32[22,7,40,128]{3,2,1,0:T(8,128)S(1)}, f32[22,3,40,128]{3,2,1,0:T(8,128)S(1)}, f32[22,8,56,128]{3,2,1,0:T(8,128)S(1)}, f32[22,8,56,128]{3,2,1,0:T(8...) custom-call(f32[16,30,128]{2,1,0:T(8,128)S(1)} %collective-permute-d, ...), custom_call_target="tpu_custom_call", output_to_operand_aliasing={{0}: (2, {}), {1}: (3, {}), {2}: (4, {}), {3}: (5, {}), {4}... | custom-call | flops 99999997952 | tf_op jit(solution)/shard_map/inner/pallas_call | solution.py:492
  22.5 0.0 collective-permute-done.4.refs_2_
  22.5 0.0 collective-permute-done.5.refs_3_
  22.6 0.0 collective-permute-done.refs_0_
  22.6 0.0 collective-permute-done.1.refs_1_
  22.6 4.6 %rim.1 = (f32[22,7,40,128]{3,2,1,0:T(8,128)S(1)}, f32[22,3,40,128]{3,2,1,0:T(8,128)S(1)}, f32[22,8,56,128]{3,2,1,0:T(8,128)S(1)}, f32[22,8,56,128]{3,2,1,0:T(8,1...) custom-call(f32[28,32,128]{2,1,0:T(8,128)S(1)} %collective-permute-d, ...), custom_call_target="tpu_custom_call", output_to_operand_aliasing={{0}: (4, {}), {1}: (5, {}), {2}: (6, {}), {3}: (7, {}), {4}... | custom-call | flops 99999997952 | tf_op jit(solution)/shard_map/rim/pallas_call | solution.py:500
  (1 shorter events, 0.0 us)
Async XLA Ops:
  1.9 9.4 %collective-permute-start.2 = (f32[16,30,128]{2,1,0:T(8,128)S(1)}, f32[16,30,128]{2,1,0:T(8,128)S(1)}, u32[]{:S(2)}, u32[]{:S(2)}) collective-permute-start(f32[16,30,128]{2,1,0:T(8,128)S(1)} %get-tuple-element.42), channel_id=1, source_target_pairs={{0,1},{1,0},{2,3},{3,2},{4,5},{5,4},{6,7},{7,6},{8,9},{9,8},{10,11... | collective-permute-start | bytes 737288 | tf_op jit(solution)/shard_map/ppermute | solution.py:50
  2.7 8.7 %collective-permute-start.3 = (f32[16,30,128]{2,1,0:T(8,128)S(1)}, f32[16,30,128]{2,1,0:T(8,128)S(1)}, u32[]{:S(2)}, u32[]{:S(2)}) collective-permute-start(f32[16,30,128]{2,1,0:T(8,128)S(1)} %get-tuple-element.43), channel_id=1, source_target_pairs={{1,2},{2,1},{5,6},{6,5},{9,10},{10,9},{13,14},{14,13},{17,18},{18,... | collective-permute-start | bytes 737288 | tf_op jit(solution)/shard_map/ppermute | solution.py:50
  5.8 16.8 %collective-permute-start = (f32[28,32,128]{2,1,0:T(8,128)S(1)}, f32[28,32,128]{2,1,0:T(8,128)S(1)}, u32[]{:S(2)}, u32[]{:S(2)}) collective-permute-start(f32[28,32,128]{2,1,0:T(8,128)S(1)} %get-tuple-element.40), channel_id=1, source_target_pairs={{4,8},{8,4},{5,9},{9,5},{6,10},{10,6},{7,11},{11,7},{20,24},{24,20... | collective-permute-start | bytes 1376264 | tf_op jit(solution)/shard_map/ppermute | solution.py:50
  9.0 13.6 %collective-permute-start.1 = (f32[28,32,128]{2,1,0:T(8,128)S(1)}, f32[28,32,128]{2,1,0:T(8,128)S(1)}, u32[]{:S(2)}, u32[]{:S(2)}) collective-permute-start(f32[28,32,128]{2,1,0:T(8,128)S(1)} %get-tuple-element.41), channel_id=1, source_target_pairs={{0,4},{4,0},{8,12},{12,8},{1,5},{5,1},{9,13},{13,9},{2,6},{6,2},{1... | collective-permute-start | bytes 1376264 | tf_op jit(solution)/shard_map/ppermute | solution.py:50
  11.4 11.1 %collective-permute-start.4 = (f32[2,2,30,128]{3,2,1,0:T(8,128)S(1)}, f32[2,2,30,128]{3,2,1,0:T(8,128)S(1)}, u32[]{:S(2)}, u32[]{:S(2)}) collective-permute-start(f32[2,2,30,128]{3,2,1,0:T(8,128)S(1)} %get-tuple-element.45), channel_id=1, source_target_pairs={{0,4},{4,0},{8,12},{12,8},{1,5},{5,1},{9,13},{13,9},{2,6},{6,2},{1... | collective-permute-start | bytes 184328 | tf_op jit(solution)/shard_map/ppermute | solution.py:50
  12.9 9.6 %collective-permute-start.5 = (f32[2,2,30,128]{3,2,1,0:T(8,128)S(1)}, f32[2,2,30,128]{3,2,1,0:T(8,128)S(1)}, u32[]{:S(2)}, u32[]{:S(2)}) collective-permute-start(f32[2,2,30,128]{3,2,1,0:T(8,128)S(1)} %get-tuple-element.46), channel_id=1, source_target_pairs={{4,8},{8,4},{5,9},{9,5},{6,10},{10,6},{7,11},{11,7},{20,24},{24,20... | collective-permute-start | bytes 184328 | tf_op jit(solution)/shard_map/ppermute | solution.py:50
